TPU v7x, 512 devices: a whole 4x4x16 slice. The times are simulated.
512 devices in a mesh: seq: 16 (over z_lo, core), chan: 32 (over x, z_hi, y).
Axes of the slice: x: 4, y: 4, z: 16 (z_hi: 2, z_lo: 8; z = z_hi * 8 + z_lo), core: 2. Of those that a mesh axis runs over, the one named last changes fastest.
Arguments:
- inner_gate: bfloat16 [2048, 8192], P('seq', 'chan'), may hold values from -6 to 6
- value_in: bfloat16 [2048, 8192], P('seq', 'chan'), may hold values from -6 to 6
- outer_gate: bfloat16 [2048, 8192], P('seq', 'chan'), may hold values from -6 to 6
- filter_taps: bfloat16 [2048, 8192], P('seq', 'chan'), may hold values from -5 to 5
- out_weight: bfloat16 [8192, 8192], P('chan'), may hold values from -0.125 to 0.125
Outputs:
- mixed: float32 [2048, 8192], P('seq', 'chan')
All inputs are finite; a program needn't handle non-finite values.
Results may differ from a plain program's by a relative error of at most 0.0029.
Values may be sent and summed in bfloat16 or wider, within the bound.
A program may use at most 64 MiB of HBM per device.

v0:
```python
import math

import jax
import jax.numpy as jnp
from jax import lax
from jax.sharding import PartitionSpec as P

TWO_PI = 2.0 * math.pi


def from_partner(block, axis, stride):
    count = lax.axis_size(axis)
    route = []
    for low in range(count):
        high = low | 1 << stride
        if high != low and high < count:
            route += [(low, high), (high, low)]
    return lax.ppermute(block, axis, route)


def turn(numerator, period):
    phase_angle = TWO_PI / period * numerator.astype(jnp.float32)
    return (jnp.cos(phase_angle), jnp.sin(phase_angle))


def dft_matrix(dft_order, orientation):
    counter = jnp.arange(dft_order, dtype=jnp.int32)
    cos_part, sin_part = turn(counter[:, None] * counter[None, :] % dft_order, dft_order)
    return (cos_part, orientation * sin_part)


def apply_dft(matrix, real_part, imag_part, pattern):
    cos_part, sin_part = matrix
    highest = lax.Precision.HIGHEST
    new_real = jnp.einsum(pattern, cos_part, real_part, precision=highest) - jnp.einsum(
        pattern, sin_part, imag_part, precision=highest
    )
    new_imag = jnp.einsum(pattern, cos_part, imag_part, precision=highest) + jnp.einsum(
        pattern, sin_part, real_part, precision=highest
    )
    return (new_real, new_imag)


def rotate_pair(real_part, imag_part, numerator, period, orientation):
    cos_part, sin_part = turn(numerator, period)
    sin_part = orientation * sin_part
    return (
        real_part * cos_part - imag_part * sin_part,
        real_part * sin_part + imag_part * cos_part,
    )


def twist(signal, position, length):
    cos_part, sin_part = turn(position, 2 * length)
    real_part = jnp.concatenate([signal, signal * cos_part], axis=-1)
    imag_part = jnp.concatenate([jnp.zeros_like(signal), -signal * sin_part], axis=-1)
    return (real_part, imag_part)


def untwist(real_part, imag_part, position, length, channels):
    cos_part, sin_part = turn(position, 2 * length)
    total = (
        real_part[..., :channels]
        + real_part[..., channels:] * cos_part
        - imag_part[..., channels:] * sin_part
    )
    return total / (2.0 * length)


def complex_product(first_real, first_imag, second_real, second_imag):
    return (
        first_real * second_real - first_imag * second_imag,
        first_real * second_imag + first_imag * second_real,
    )


def local(inner_gate, value_in, outer_gate, filter_taps, out_weight):
    tok_rows, channels = inner_gate.shape
    seq_devices = lax.axis_size("seq")
    length = tok_rows * seq_devices
    device_index = lax.axis_index("seq")
    section_count = seq_devices.bit_length() - 1
    row_index = jnp.arange(tok_rows, dtype=jnp.int32)[:, None]
    position = device_index * tok_rows + row_index
    signal = inner_gate.astype(jnp.float32) * value_in.astype(jnp.float32)
    kernel = filter_taps.astype(jnp.float32)
    sig_real, sig_imag = twist(signal, position, length)
    ker_real, ker_imag = twist(kernel, position, length)
    stacked = jnp.stack([jnp.stack([sig_real, ker_real]), jnp.stack([sig_imag, ker_imag])])
    for section_bit in reversed(range(section_count)):
        span_half = 1 << section_bit
        partner = from_partner(stacked, "seq", section_bit)
        is_upper = device_index >> section_bit & 1
        cos_part, sin_part = turn(device_index & span_half - 1, 2 * span_half)
        difference = partner - stacked
        turned = jnp.stack(
            [
                difference[0] * cos_part + difference[1] * sin_part,
                difference[1] * cos_part - difference[0] * sin_part,
            ]
        )
        stacked = jnp.where(is_upper == 1, turned, stacked + partner)
    reversed_index = jnp.zeros((), jnp.int32)
    for digit in range(section_count):
        reversed_index = reversed_index + ((device_index >> digit & 1) << section_count - 1 - digit)
    twiddle_num = row_index * reversed_index % length
    spec_real, spec_imag = rotate_pair(stacked[0], stacked[1], twiddle_num, length, -1.0)
    spec_real, spec_imag = apply_dft(
        dft_matrix(tok_rows, -1.0), spec_real, spec_imag, "kr,srf->skf"
    )
    prod_real, prod_imag = complex_product(spec_real[0], spec_imag[0], spec_real[1], spec_imag[1])
    prod_real, prod_imag = apply_dft(dft_matrix(tok_rows, 1.0), prod_real, prod_imag, "kr,rf->kf")
    prod_real, prod_imag = rotate_pair(prod_real, prod_imag, twiddle_num, length, 1.0)
    current = jnp.stack([prod_real, prod_imag])
    for section_bit in range(section_count):
        span_half = 1 << section_bit
        partner = from_partner(current, "seq", section_bit)
        is_upper = device_index >> section_bit & 1
        cos_part, sin_part = turn(device_index & span_half - 1, 2 * span_half)
        spun_mine = jnp.stack(
            [
                current[0] * cos_part - current[1] * sin_part,
                current[0] * sin_part + current[1] * cos_part,
            ]
        )
        spun_partner = jnp.stack(
            [
                partner[0] * cos_part - partner[1] * sin_part,
                partner[0] * sin_part + partner[1] * cos_part,
            ]
        )
        current = jnp.where(is_upper == 1, partner - spun_mine, current + spun_partner)
    convolved = untwist(current[0], current[1], position, length, channels)
    gated = (outer_gate.astype(jnp.float32) * convolved).astype(jnp.bfloat16)
    partials = jnp.dot(gated, out_weight, preferred_element_type=jnp.float32)
    mixed = lax.psum_scatter(partials, "chan", scatter_dimension=1, tiled=True)
    return mixed


def solution(mesh):
    in_specs = (
        P("seq", "chan"),
        P("seq", "chan"),
        P("seq", "chan"),
        P("seq", "chan"),
        P("chan", None),
    )
    out_specs = P("seq", "chan")
    return jax.shard_map(local, mesh=mesh, in_specs=in_specs, out_specs=out_specs, check_vma=False)
```

profile of v0, /device:TPU:160, one launch (start us, length us, event | category | flops | bytes accessed | tf_op | source)
XLA Modules:
  0.0 682.1 jit_solution(16825043553379380739)
XLA Ops:
  6.6 0.9 convert_element_type.83
  7.4 1.0 convert_multiply_fusion
  8.6 0.1 pad_maximum_fusion
  8.7 1.9 collective-permute-start
  10.8 67.5 %collective-permute-done = f32[2,2,128,512]{3,2,1,0:T(8,128)S(1)} collective-permute-done((f32[2,2,128,512]{3,2,1,0:T(8,128)S(1)}, f32[2,2,128,512]{3,2,1,0:T(8,128)S(1)}, u32[]{:S(2)}, u32[]{:S(2)}) %collective-permute-start) | collective-permute-done | bytes 1048608 | tf_op jit(solution)/shard_map/ppermute | solution.py:18
  78.3 0.2 fusion.90
  78.5 0.2 multiply_add_fusion.4
  78.7 1.3 maximum_select_fusion
  80.0 32.4 %collective-permute-start.1 = (f32[2,2,128,512]{3,2,1,0:T(8,128)}, f32[2,2,128,512]{3,2,1,0:T(8,128)}, u32[]{:S(2)}, u32[]{:S(2)}) collective-permute-start(f32[2,2,128,512]{3,2,1,0:T(8,128)} %maximum_select_fusion), channel_id=1, source_target_pairs={{0,128},{128,0},{32,160},{160,32},{64,192},{192,64},{96,224},{224,... | collective-permute-start | bytes 3145736 | tf_op jit(solution)/shard_map/ppermute | solution.py:18
  112.6 37.8 %collective-permute-done.1 = f32[2,2,128,512]{3,2,1,0:T(8,128)} collective-permute-done((f32[2,2,128,512]{3,2,1,0:T(8,128)}, f32[2,2,128,512]{3,2,1,0:T(8,128)}, u32[]{:S(2)}, u32[]{:S(2)}) %collective-permute-start.1) | collective-permute-done | bytes 1048608 | tf_op jit(solution)/shard_map/ppermute | solution.py:18
  150.4 1.7 fusion.96
  152.1 0.2 multiply_add_fusion.3
  152.3 2.1 maximum_select_fusion.1
  154.5 3.3 collective-permute-start.2
  157.9 23.5 %collective-permute-done.2 = f32[2,2,128,512]{3,2,1,0:T(8,128)S(1)} collective-permute-done((f32[2,2,128,512]{3,2,1,0:T(8,128)S(1)}, f32[2,2,128,512]{3,2,1,0:T(8,128)S(1)}, u32[]{:S(2)}, u32[]{:S(2)}) %collective-permute-start.2) | collective-permute-done | bytes 1048608 | tf_op jit(solution)/shard_map/ppermute | solution.py:18
  181.4 0.2 sub.99
  181.7 0.1 multiply_add_fusion.2
  181.8 0.4 maximum_select_fusion.2
  182.2 2.1 collective-permute-start.3
  184.4 2.3 collective-permute-done.3
  186.7 0.2 sub.101
  186.9 0.1 multiply_add_fusion.1
  187.1 0.4 maximum_select_fusion.3
  187.4 1.2 fusion.26
  188.6 1.2 fusion.24
  189.9 1.2 fusion.1
  191.1 1.2 fusion
  192.4 0.6 fusion.6
  193.0 0.6 fusion.10
  193.7 0.7 convolution_add_fusion.1
  194.3 0.7 subtract_bitcast_fusion
  195.1 2.0 collective-permute-start.4
  197.2 1.7 collective-permute-done.4
  199.0 0.2 fusion.2
  199.2 2.2 collective-permute-start.5
  201.4 0.1 multiply_subtract_fusion.10
  201.5 13.6 %collective-permute-done.5 = f32[2,128,512]{2,1,0:T(8,128)S(1)} collective-permute-done((f32[2,128,512]{2,1,0:T(8,128)S(1)}, f32[2,128,512]{2,1,0:T(8,128)S(1)}, u32[]{:S(2)}, u32[]{:S(2)}) %collective-permute-start.5) | collective-permute-done | bytes 524320 | tf_op jit(solution)/shard_map/ppermute | solution.py:18
  215.1 0.4 fusion.3
  215.6 5.3 collective-permute-start.6
  220.9 0.1 multiply_subtract_fusion.8
  220.9 21.5 %collective-permute-done.6 = f32[2,128,512]{2,1,0:T(8,128)S(1)} collective-permute-done((f32[2,128,512]{2,1,0:T(8,128)S(1)}, f32[2,128,512]{2,1,0:T(8,128)S(1)}, u32[]{:S(2)}, u32[]{:S(2)}) %collective-permute-start.6) | collective-permute-done | bytes 524320 | tf_op jit(solution)/shard_map/ppermute | solution.py:18
  242.6 0.2 fusion.4
  242.8 6.3 collective-permute-start.7
  249.1 0.1 multiply_subtract_fusion.6
  249.2 33.8 %collective-permute-done.7 = f32[2,128,512]{2,1,0:T(8,128)S(1)} collective-permute-done((f32[2,128,512]{2,1,0:T(8,128)S(1)}, f32[2,128,512]{2,1,0:T(8,128)S(1)}, u32[]{:S(2)}, u32[]{:S(2)}) %collective-permute-start.7) | collective-permute-done | bytes 524320 | tf_op jit(solution)/shard_map/ppermute | solution.py:18
  283.0 0.2 fusion.5
  283.3 2.7 fusion.20
  286.1 389.2 %reduce-scatter.2.cloned.1.call-done = f32[128,256]{1,0:T(8,128)} async-done(((f32[128,8192]{1,0:T(8,128)}), f32[128,256]{1,0:T(8,128)}) %reduce-scatter.2.cloned.1.call-update) | async-done | bytes 131088 | tf_op jit(solution)/shard_map/reduce_scatter | solution.py:136
  (27 shorter events, 0.8 us)
Async XLA Ops:
  6.5 668.7 %reduce-scatter.2.cloned.1.call-start = ((), (), s32[]{:S(2)}) async-start(), calls=%async_computation.1 | async-start | bytes 4325376 | tf_op jit(solution)/shard_map/reduce_scatter | solution.py:136
  8.7 69.6 %collective-permute-start = (f32[2,2,128,512]{3,2,1,0:T(8,128)S(1)}, f32[2,2,128,512]{3,2,1,0:T(8,128)S(1)}, u32[]{:S(2)}, u32[]{:S(2)}) collective-permute-start(f32[2,2,128,512]{3,2,1,0:T(8,128)S(1)} %pad_maximum_fusion), channel_id=1, source_target_pairs={{0,256},{256,0},{32,288},{288,32},{64,320},{320,64},{96,352},{352,... | collective-permute-start | bytes 3145736 | tf_op jit(solution)/shard_map/ppermute | solution.py:18
  78.7 73.4 %copy-start = (f32[1,2,128,512]{3,2,1,0:T(8,128)}, f32[1,2,128,512]{3,2,1,0:T(8,128)S(1)}, u32[]{:S(2)}) copy-start(f32[1,2,128,512]{3,2,1,0:T(8,128)S(1)} %get-tuple-element.16) | copy-start | bytes 1572868
  78.7 73.4 %copy-start.1 = (f32[1,2,128,512]{3,2,1,0:T(8,128)}, f32[1,2,128,512]{3,2,1,0:T(8,128)S(1)}, u32[]{:S(2)}) copy-start(f32[1,2,128,512]{3,2,1,0:T(8,128)S(1)} %get-tuple-element.17) | copy-start | bytes 1572868
  80.0 70.4 %collective-permute-start.1 = (f32[2,2,128,512]{3,2,1,0:T(8,128)}, f32[2,2,128,512]{3,2,1,0:T(8,128)}, u32[]{:S(2)}, u32[]{:S(2)}) collective-permute-start(f32[2,2,128,512]{3,2,1,0:T(8,128)} %maximum_select_fusion), channel_id=1, source_target_pairs={{0,128},{128,0},{32,160},{160,32},{64,192},{192,64},{96,224},{224,... | collective-permute-start | bytes 3145736 | tf_op jit(solution)/shard_map/ppermute | solution.py:18
  154.5 27.0 %collective-permute-start.2 = (f32[2,2,128,512]{3,2,1,0:T(8,128)S(1)}, f32[2,2,128,512]{3,2,1,0:T(8,128)S(1)}, u32[]{:S(2)}, u32[]{:S(2)}) collective-permute-start(f32[2,2,128,512]{3,2,1,0:T(8,128)S(1)} %maximum_select_fusion.1), channel_id=1, source_target_pairs={{0,64},{64,0},{32,96},{96,32},{128,192},{192,128},{160,224},{224,1... | collective-permute-start | bytes 3145736 | tf_op jit(solution)/shard_map/ppermute | solution.py:18
  182.2 4.6 collective-permute-start.3
  195.1 3.8 collective-permute-start.4
  199.2 15.9 %collective-permute-start.5 = (f32[2,128,512]{2,1,0:T(8,128)S(1)}, f32[2,128,512]{2,1,0:T(8,128)S(1)}, u32[]{:S(2)}, u32[]{:S(2)}) collective-permute-start(f32[2,128,512]{2,1,0:T(8,128)S(1)} %fusion.2), channel_id=1, source_target_pairs={{0,64},{64,0},{32,96},{96,32},{128,192},{192,128},{160,224},{224,1... | collective-permute-start | bytes 1572872 | tf_op jit(solution)/shard_map/ppermute | solution.py:18
  215.6 26.9 %collective-permute-start.6 = (f32[2,128,512]{2,1,0:T(8,128)S(1)}, f32[2,128,512]{2,1,0:T(8,128)S(1)}, u32[]{:S(2)}, u32[]{:S(2)}) collective-permute-start(f32[2,128,512]{2,1,0:T(8,128)S(1)} %fusion.3), channel_id=1, source_target_pairs={{0,128},{128,0},{32,160},{160,32},{64,192},{192,64},{96,224},{224,... | collective-permute-start | bytes 1572872 | tf_op jit(solution)/shard_map/ppermute | solution.py:18
  242.5 40.8 %copy-start.2 = (bf16[256,8192]{1,0:T(8,128)(2,1)S(1)}, bf16[256,8192]{1,0:T(8,128)(2,1)}, u32[]{:S(2)}) copy-start(bf16[256,8192]{1,0:T(8,128)(2,1)} %param.9) | copy-start | bytes 12582916
  242.5 40.8 %copy-start.3 = (bf16[128,256]{1,0:T(8,128)(2,1)S(1)}, bf16[128,256]{1,0:T(8,128)(2,1)}, u32[]{:S(2)}) copy-start(bf16[128,256]{1,0:T(8,128)(2,1)} %param.7) | copy-start | bytes 196612
  242.8 40.2 %collective-permute-start.7 = (f32[2,128,512]{2,1,0:T(8,128)S(1)}, f32[2,128,512]{2,1,0:T(8,128)S(1)}, u32[]{:S(2)}, u32[]{:S(2)}) collective-permute-start(f32[2,128,512]{2,1,0:T(8,128)S(1)} %fusion.4), channel_id=1, source_target_pairs={{0,256},{256,0},{32,288},{288,32},{64,320},{320,64},{96,352},{352,... | collective-permute-start | bytes 1572872 | tf_op jit(solution)/shard_map/ppermute | solution.py:18
Sparse Core Ops, SparseCore 0:
  286.2 388.9 reduce-scatter.1
where the time goes:
time: 683 us; the launch traced here: 682 us
  waiting for transfers between devices  591 us (87%)
  starting transfers between devices  55.6 us (8%)
  between operations  14.3 us (2%)
  other arithmetic  11 us (2%)
  matrix products  10.2 us (1%)
    reduce_scatter x1, waiting for transfers between devices, local(): mixed = lax.psum_scatter(partials, 'chan', scatter_dimension=1, tiled=True)  389 us
    ppermute x8, waiting for transfers between devices, from_partner(): return lax.ppermute(block, axis, route)  202 us
    ppermute x8, starting transfers between devices, from_partner(): return lax.ppermute(block, axis, route)  55.6 us
  transfers between devices with their start and end apart: 9, of which 9 were waited for; matrix products, arithmetic and copies ran while one was open for 0% of the time, Pallas kernels for 0%

commit v1 on v0

v1 whole, which is shorter than its diff:
```python
import functools

import jax
import jax.numpy as jnp
import ml_dtypes
import numpy as np
from jax import lax
from jax.experimental import pallas as pl
from jax.experimental.pallas import tpu as pltpu
from jax.sharding import PartitionSpec as P

MESH = pl.DeviceIdType.MESH
NX, NZ, NY = 4, 2, 4
F32, BF16 = jnp.float32, jnp.bfloat16


def split_bf16(values):
    high = values.astype(ml_dtypes.bfloat16)
    low = (values - high.astype(np.float64)).astype(ml_dtypes.bfloat16)
    return np.stack([high, low])


@functools.lru_cache(None)
def transform_constants(blocks, rows, group):
    j, b = np.arange(blocks), np.arange(rows)
    eye = np.eye(group)
    angle = 2 * np.pi * ((4 * j[:, None] + 1) * j[None, :] % (4 * blocks)) / (4 * blocks)
    f1 = np.concatenate([np.kron(np.cos(angle), eye), np.kron(-np.sin(angle), eye)], 0)
    f2 = np.concatenate([np.kron(np.cos(angle).T, eye), np.kron(np.sin(angle).T, eye)], 1) / (blocks * rows)
    turn = 2 * np.pi * ((4 * j[:, None] + 1) * b[None, :]) / (4 * blocks * rows)
    tw = np.stack([np.repeat(np.cos(turn), group, 0), np.repeat(np.sin(turn), group, 0)]).astype(np.float32)
    inner = 2 * np.pi * (b[:, None] * b[None, :] % rows) / rows
    c, s = np.cos(inner), np.sin(inner)
    g = np.block([[c, -s], [s, c]])
    return split_bf16(f1), split_bf16(f2), split_bf16(g), tw


def halves(value):
    high = value.astype(BF16)
    return high, (value - high.astype(F32)).astype(BF16)


def mm(a, b):
    return jnp.dot(a, b, preferred_element_type=F32)


def convolve(hi, lo, taps, f1, f2, g, tw):
    n, rows = hi.shape
    g_hi, g_lo = g[0], g[1]
    cos, sin = tw[0], tw[1]

    def within(re, im):
        high, low = halves(jnp.concatenate([re, im], 1))
        return mm(high, g_hi) + (mm(low, g_hi) + mm(high, g_lo))

    both = jnp.concatenate([hi, taps], 1)
    first = mm(f1[0], both) + mm(f1[1], both)
    sig = first[:, :rows] + mm(f1[0], lo)
    ker = first[:, rows:]

    def turned(re, im):
        return re * cos + im * sin, im * cos - re * sin

    s_re, s_im = turned(sig[:n], sig[n:])
    k_re, k_im = turned(ker[:n], ker[n:])
    spec = within(jnp.concatenate([s_re, k_re], 0), jnp.concatenate([s_im, k_im], 0))
    s_re, s_im = spec[:n, :rows], spec[:n, rows:]
    k_re, k_im = spec[n:, :rows], spec[n:, rows:]
    p_re = s_re * k_re - s_im * k_im
    p_im = -(s_re * k_im + s_im * k_re)
    back = within(p_re, p_im)
    w_re, w_im = turned(back[:, :rows], back[:, rows:])
    high, low = halves(jnp.concatenate([w_re, w_im], 0))
    out = mm(f2[0], jnp.concatenate([high, low], 1))
    return out[:, :rows] + (out[:, rows:] + mm(f2[1], high))


def kernel(
    inner_ref, value_ref, outer_ref, taps_ref, w_hbm, f1_hbm, f2_hbm, g_hbm, tw_hbm, out_ref,
    send, send_o, got, got_o, send_g, got_g, w, f1, f2, g, tw, acc, s1, r1, s2, r2, zs, zr,
    load_sem, a_ss, a_rs, o_ss, o_rs, g_ss, g_rs, s1_ss, s1_rs, s2_ss, s2_rs, z_ss, z_rs,
):
    seq = lax.axis_size("seq")
    me, chan = lax.axis_index("seq"), lax.axis_index("chan")
    x, zh, y = chan // (NZ * NY), chan // NY % NZ, chan % NY
    rows, channels = inner_ref.shape
    group = channels // seq
    half = rows // 2

    def at(dx, dz, dy):
        return ((x + dx) % NX * NZ + (zh + dz) % NZ) * NY + (y + dy) % NY

    loads = [
        pltpu.make_async_copy(src, dst, load_sem.at[i])
        for i, (src, dst) in enumerate([(f1_hbm, f1), (f2_hbm, f2), (g_hbm, g), (tw_hbm, tw), (w_hbm, w)])
    ]
    for load in loads:
        load.start()

    others = [(lax.rem(me + k, seq), chan) for k in range(1, seq)]
    others += [(me, at(d, 0, 0)) for d in range(1, NX)] + [(me, at(0, 0, d)) for d in range(1, NY)] + [(me, at(0, 1, 0))]
    barrier = pltpu.get_barrier_semaphore()
    for other in others:
        pl.semaphore_signal(barrier, inc=1, device_id=other, device_id_type=MESH)

    signal = (inner_ref[...].astype(F32) * value_ref[...].astype(F32)).T
    hi, lo = halves(signal)
    send[:, 0:group] = hi.reshape(seq, group, rows)
    send[:, group : 2 * group] = lo.reshape(seq, group, rows)
    send[:, 2 * group : 3 * group] = taps_ref[...].astype(F32).T.astype(BF16).reshape(seq, group, rows)
    send_o[...] = outer_ref[...].astype(F32).T.astype(BF16).reshape(seq, group, rows)
    pl.semaphore_wait(barrier, len(others))

    def spread(src, dst, ss, rs):
        copies = []
        for k in range(1, seq):
            to = lax.rem(me + k, seq)
            copy = pltpu.make_async_remote_copy(
                src_ref=src.at[to], dst_ref=dst.at[me], send_sem=ss.at[k - 1], recv_sem=rs.at[k - 1],
                device_id=(to, chan), device_id_type=MESH,
            )
            copy.start()
            copies.append(copy)
        return copies

    out_a = spread(send, got, a_ss, a_rs)
    out_o = spread(send_o, got_o, o_ss, o_rs)
    got[me] = send[me]
    got_o[me] = send_o[me]
    for load in loads[:4]:
        load.wait()
    for copy in out_a:
        copy.wait_recv()
    n = seq * group
    conv = convolve(
        got[:, 0:group].reshape(n, rows), got[:, group : 2 * group].reshape(n, rows),
        got[:, 2 * group : 3 * group].reshape(n, rows), f1, f2, g, tw,
    )
    for copy in out_o:
        copy.wait_recv()
    gated = (got_o[...].reshape(n, rows).astype(F32) * conv).astype(BF16)
    send_g[...] = gated.reshape(seq, group, rows)
    out_g = spread(send_g, got_g, g_ss, g_rs)
    got_g[me] = send_g[me]
    loads[4].wait()
    for copy in out_g:
        copy.wait_recv()
    mine = got_g[...].reshape(n, rows).astype(F32).T.astype(BF16)

    width = channels

    def remote(src, dst, ss, rs, dx, dz, dy):
        copy = pltpu.make_async_remote_copy(
            src_ref=src, dst_ref=dst, send_sem=ss, recv_sem=rs, device_id=(me, at(dx, dz, dy)), device_id_type=MESH
        )
        copy.start()
        return copy

    order = [2, 1, 3, 0]
    sent = []
    stage1 = {}
    for wave in range(2):
        dz = 1 - wave
        done = set()
        for first in order:
            todo = [(first, d) for d in order] + [(d, first) for d in order]
            for dx, dy in todo:
                if (dx, dy) in done:
                    continue
                done.add((dx, dy))
                column = pl.multiple_of(at(dx, dz, dy) * width, width)
                block = mm(mine, w[:, pl.ds(column, width)])
                if dx == 0:
                    acc[wave, 0, :, dy * width : (dy + 1) * width] = block[:half]
                else:
                    s1[wave, 0, dx - 1, :, dy * width : (dy + 1) * width] = block[:half].astype(BF16)
                if dy == 0:
                    acc[wave, 1, :, dx * width : (dx + 1) * width] = block[half:]
                else:
                    s1[wave, 1, dy - 1, :, dx * width : (dx + 1) * width] = block[half:].astype(BF16)
            if first:
                for h in range(2):
                    stage1[wave, h, first] = remote(
                        s1.at[wave, h, first - 1], r1.at[wave, h, first - 1],
                        s1_ss.at[wave, h, first - 1], s1_rs.at[wave, h, first - 1],
                        first * (1 - h), 0, first * h,
                    )
    last = []
    for wave in range(2):
        stage2 = {}
        for h in range(2):
            for d in (1, 3, 2):
                stage1[wave, h, d].wait_recv()
            for d in order:
                cols = slice(d * width, (d + 1) * width)
                total = acc[wave, h, :, cols]
                for e in range(3):
                    total = total + r1[wave, h, e, :, cols].astype(F32)
                if d:
                    s2[wave, h, d - 1] = total.astype(BF16)
                    stage2[h, d] = remote(
                        s2.at[wave, h, d - 1], r2.at[wave, h, d - 1],
                        s2_ss.at[wave, h, d - 1], s2_rs.at[wave, h, d - 1], d * h, 0, d * (1 - h),
                    )
                else:
                    acc[wave, h, :, cols] = total
        sent += list(stage2.values())
        for h in range(2):
            total = acc[wave, h, :, 0:width]
            for d in (1, 3, 2):
                stage2[h, d].wait_recv()
                total = total + r2[wave, h, d - 1].astype(F32)
            if wave == 0:
                zs[h] = total.astype(BF16)
                last.append(remote(zs.at[h], zr.at[h], z_ss.at[h], z_rs.at[h], 0, 1, 0))
            else:
                last[h].wait_recv()
                out_ref[h * half : (h + 1) * half, :] = total + zr[h].astype(F32)
    for copy in out_a + out_o + out_g + list(stage1.values()) + sent + last:
        copy.wait_send()


def local(inner_gate, value_in, outer_gate, filter_taps, out_weight):
    rows, channels = inner_gate.shape
    seq = lax.axis_size("seq")
    group, half = channels // seq, rows // 2
    f1, f2, g, tw = transform_constants(seq, rows, group)
    vmem, dma = pltpu.VMEM, pltpu.SemaphoreType.DMA
    in_vmem = pl.BlockSpec(memory_space=pltpu.VMEM)
    in_any = pl.BlockSpec(memory_space=pl.ANY)
    peers = seq - 1
    scratch = [
        vmem((seq, 3 * group, rows), BF16), vmem((seq, group, rows), BF16),
        vmem((seq, 3 * group, rows), BF16), vmem((seq, group, rows), BF16),
        vmem((seq, group, rows), BF16), vmem((seq, group, rows), BF16),
        vmem(out_weight.shape, BF16), vmem(f1.shape, BF16), vmem(f2.shape, BF16), vmem(g.shape, BF16), vmem(tw.shape, F32),
        vmem((2, 2, half, 4 * channels), F32),
        vmem((2, 2, 3, half, 4 * channels), BF16), vmem((2, 2, 3, half, 4 * channels), BF16),
        vmem((2, 2, 3, half, channels), BF16), vmem((2, 2, 3, half, channels), BF16),
        vmem((2, half, channels), BF16), vmem((2, half, channels), BF16),
        dma((5,)), dma((peers,)), dma((peers,)), dma((peers,)), dma((peers,)), dma((peers,)), dma((peers,)),
        dma((2, 2, 3)), dma((2, 2, 3)), dma((2, 2, 3)), dma((2, 2, 3)), dma((2,)), dma((2,)),
    ]
    return pl.pallas_call(
        kernel,
        out_shape=jax.ShapeDtypeStruct((rows, channels), F32),
        in_specs=[in_vmem] * 4 + [in_any] * 5,
        out_specs=in_vmem,
        scratch_shapes=scratch,
        compiler_params=pltpu.CompilerParams(collective_id=0, has_side_effects=True, vmem_limit_bytes=48 * 2**20),
        name="hyena",
    )(inner_gate, value_in, outer_gate, filter_taps, out_weight, *(jnp.asarray(c) for c in (f1, f2, g, tw)))


def solution(mesh):
    in_specs = (P("seq", "chan"),) * 4 + (P("chan", None),)
    return jax.shard_map(local, mesh=mesh, in_specs=in_specs, out_specs=P("seq", "chan"), check_vma=False)
```

time: 683 us -> 74.3 us (0.11)
  the two profiles are of different devices: /device:TPU:160 before, /device:TPU:32 now
where the time goes in v1:
time: 74.3 us; the launch traced here: 73.8 us
  Pallas kernels  63.6 us (86%)
  local copies, waits for them, and re-layouts  10.2 us (14%)
    pallas_call x1, Pallas kernels, local(): pl.pallas_call(kernel, out_shape=jax.ShapeDtypeStruct((rows, channels), F...  63.6 us
    unnamed x19, local copies, waits for them, and re-layouts  10.2 us

profile of v1, /device:TPU:32, one launch (start us, length us, event | category | flops | bytes accessed | tf_op | source)
XLA Modules:
  0.0 73.8 jit_solution(1353278007781909522)
XLA Ops:
  0.0 0.0 copy-start
  0.0 2.2 %copy-done = bf16[256,8192]{1,0:T(8,128)(2,1)S(1)} copy-done((bf16[256,8192]{1,0:T(8,128)(2,1)S(1)}, bf16[256,8192]{1,0:T(8,128)(2,1)}, u32[]{:S(2)}) %copy-start) | copy-done | bytes 4194328
  2.2 0.0 copy-start.1
  2.2 1.0 %copy-done.1 = bf16[2,256,512]{2,1,0:T(8,128)(2,1)S(1)} copy-done((bf16[2,256,512]{2,1,0:T(8,128)(2,1)S(1)}, bf16[2,256,512]{2,1,0:T(8,128)(2,1)}, u32[]{:S(2)}) %copy-start.1) | copy-done | bytes 524312
  3.2 0.0 copy-start.2
  3.2 1.0 %copy-done.2 = bf16[2,512,256]{2,1,0:T(8,128)(2,1)S(1)} copy-done((bf16[2,512,256]{2,1,0:T(8,128)(2,1)S(1)}, bf16[2,512,256]{2,1,0:T(8,128)(2,1)}, u32[]{:S(2)}) %copy-start.2) | copy-done | bytes 524312
  4.3 0.0 copy-start.3
  4.3 0.9 %copy-done.3 = f32[2,256,128]{2,1,0:T(8,128)S(1)} copy-done((f32[2,256,128]{2,1,0:T(8,128)S(1)}, f32[2,256,128]{2,1,0:T(8,128)}, u32[]{:S(2)}) %copy-start.3) | copy-done | bytes 262168
  5.2 0.0 copy-start.4
  5.2 0.9 %copy-done.4 = bf16[2,256,256]{2,1,0:T(8,128)(2,1)S(1)} copy-done((bf16[2,256,256]{2,1,0:T(8,128)(2,1)S(1)}, bf16[2,256,256]{2,1,0:T(8,128)(2,1)}, u32[]{:S(2)}) %copy-start.4) | copy-done | bytes 262168
  6.2 0.0 copy-start.5
  6.2 0.8 %copy-done.5 = bf16[128,256]{1,0:T(8,128)(2,1)S(1)} copy-done((bf16[128,256]{1,0:T(8,128)(2,1)S(1)}, bf16[128,256]{1,0:T(8,128)(2,1)}, u32[]{:S(2)}) %copy-start.5) | copy-done | bytes 65560
  7.0 0.0 copy-start.6
  7.0 0.8 %copy-done.6 = bf16[128,256]{1,0:T(8,128)(2,1)S(1)} copy-done((bf16[128,256]{1,0:T(8,128)(2,1)S(1)}, bf16[128,256]{1,0:T(8,128)(2,1)}, u32[]{:S(2)}) %copy-start.6) | copy-done | bytes 65560
  7.9 0.0 copy-start.7
  7.9 0.8 %copy-done.7 = bf16[128,256]{1,0:T(8,128)(2,1)S(1)} copy-done((bf16[128,256]{1,0:T(8,128)(2,1)S(1)}, bf16[128,256]{1,0:T(8,128)(2,1)}, u32[]{:S(2)}) %copy-start.7) | copy-done | bytes 65560
  8.7 0.0 copy-start.8
  8.7 0.8 %copy-done.8 = bf16[128,256]{1,0:T(8,128)(2,1)S(1)} copy-done((bf16[128,256]{1,0:T(8,128)(2,1)S(1)}, bf16[128,256]{1,0:T(8,128)(2,1)}, u32[]{:S(2)}) %copy-start.8) | copy-done | bytes 65560
  9.5 63.6 %hyena.1 = f32[128,256]{1,0:T(8,128)S(1)} custom-call(bf16[128,256]{1,0:T(8,128)(2,1)S(1)} %copy-done.5, bf16[128,256]{1,0:T(8,128)(2,1)S(1)} %copy-done.6, bf16[128,256]{1,0:T(8,128)(2,1)S(1)} %copy-done.7, bf16[128,256]{1,0:T(8,128)(2,1)S(1)} %copy-done.8, bf16[256,8192]{1,0:T(8,128)(2,1)S(1)} %copy-done, bf16[2,512,256]{2,1,0:T(8,128)(2,1)S(1)} %copy-done.2, ...), custom_call_target="tpu_custom_call" | custom-call | tf_op jit(solution)/shard_map/hyena/pallas_call | solution.py:244
  73.2 0.7 copy.11
Async XLA Ops:
  0.0 2.2 %copy-start = (bf16[256,8192]{1,0:T(8,128)(2,1)S(1)}, bf16[256,8192]{1,0:T(8,128)(2,1)}, u32[]{:S(2)}) copy-start(bf16[256,8192]{1,0:T(8,128)(2,1)} %w_hbm.1) | copy-start | bytes 12582916
  2.2 1.0 %copy-start.1 = (bf16[2,256,512]{2,1,0:T(8,128)(2,1)S(1)}, bf16[2,256,512]{2,1,0:T(8,128)(2,1)}, u32[]{:S(2)}) copy-start(bf16[2,256,512]{2,1,0:T(8,128)(2,1)} %constant.9.clone.f2_hbm) | copy-start | bytes 1572868
  3.2 1.0 %copy-start.2 = (bf16[2,512,256]{2,1,0:T(8,128)(2,1)S(1)}, bf16[2,512,256]{2,1,0:T(8,128)(2,1)}, u32[]{:S(2)}) copy-start(bf16[2,512,256]{2,1,0:T(8,128)(2,1)} %constant.8.clone.f1_hbm) | copy-start | bytes 1572868
  4.3 0.9 %copy-start.3 = (f32[2,256,128]{2,1,0:T(8,128)S(1)}, f32[2,256,128]{2,1,0:T(8,128)}, u32[]{:S(2)}) copy-start(f32[2,256,128]{2,1,0:T(8,128)} %constant.11.clone.tw_hbm) | copy-start | bytes 786436
  5.2 0.9 %copy-start.4 = (bf16[2,256,256]{2,1,0:T(8,128)(2,1)S(1)}, bf16[2,256,256]{2,1,0:T(8,128)(2,1)}, u32[]{:S(2)}) copy-start(bf16[2,256,256]{2,1,0:T(8,128)(2,1)} %constant.10.clone.g_hbm) | copy-start | bytes 786436
  6.2 0.8 %copy-start.5 = (bf16[128,256]{1,0:T(8,128)(2,1)S(1)}, bf16[128,256]{1,0:T(8,128)(2,1)}, u32[]{:S(2)}) copy-start(bf16[128,256]{1,0:T(8,128)(2,1)} %inner_ref.1) | copy-start | bytes 196612
  7.0 0.8 %copy-start.6 = (bf16[128,256]{1,0:T(8,128)(2,1)S(1)}, bf16[128,256]{1,0:T(8,128)(2,1)}, u32[]{:S(2)}) copy-start(bf16[128,256]{1,0:T(8,128)(2,1)} %value_ref.1) | copy-start | bytes 196612
  7.9 0.8 %copy-start.7 = (bf16[128,256]{1,0:T(8,128)(2,1)S(1)}, bf16[128,256]{1,0:T(8,128)(2,1)}, u32[]{:S(2)}) copy-start(bf16[128,256]{1,0:T(8,128)(2,1)} %outer_ref.1) | copy-start | bytes 196612
  8.7 0.8 %copy-start.8 = (bf16[128,256]{1,0:T(8,128)(2,1)S(1)}, bf16[128,256]{1,0:T(8,128)(2,1)}, u32[]{:S(2)}) copy-start(bf16[128,256]{1,0:T(8,128)(2,1)} %taps_ref.1) | copy-start | bytes 196612

commit v2 on v1

--- a/solution.py
+++ b/solution.py
@@ -76,40 +76,54 @@
 
 
 def kernel(
-    inner_ref, value_ref, outer_ref, taps_ref, w_hbm, f1_hbm, f2_hbm, g_hbm, tw_hbm, out_ref,
-    send, send_o, got, got_o, send_g, got_g, w, f1, f2, g, tw, acc, s1, r1, s2, r2, zs, zr,
-    load_sem, a_ss, a_rs, o_ss, o_rs, g_ss, g_rs, s1_ss, s1_rs, s2_ss, s2_rs, z_ss, z_rs,
+    inner_hbm, value_hbm, outer_hbm, taps_hbm, w_hbm, f1_hbm, f2_hbm, g_hbm, tw_hbm, own_hbm, far_hbm,
+    inner_ref, value_ref, outer_ref, taps_ref, send, send_o, got, got_o, send_g, got_g, w, f1, f2, g, tw, acc, s1, r1, s2, r2, zs, own,
+    load_sem, own_sem, far_sem, a_ss, a_rs, o_ss, o_rs, g_ss, g_rs, s1_ss, s1_rs, s2_ss, s2_rs, z_ss, z_rs,
 ):
     seq = lax.axis_size("seq")
     me, chan = lax.axis_index("seq"), lax.axis_index("chan")
     x, zh, y = chan // (NZ * NY), chan // NY % NZ, chan % NY
-    rows, channels = inner_ref.shape
+    rows, channels = own_hbm.shape
     group = channels // seq
     half = rows // 2
 
     def at(dx, dz, dy):
         return ((x + dx) % NX * NZ + (zh + dz) % NZ) * NY + (y + dy) % NY
 
-    loads = [
-        pltpu.make_async_copy(src, dst, load_sem.at[i])
-        for i, (src, dst) in enumerate([(f1_hbm, f1), (f2_hbm, f2), (g_hbm, g), (tw_hbm, tw), (w_hbm, w)])
-    ]
-    for load in loads:
-        load.start()
-
     others = [(lax.rem(me + k, seq), chan) for k in range(1, seq)]
-    others += [(me, at(d, 0, 0)) for d in range(1, NX)] + [(me, at(0, 0, d)) for d in range(1, NY)] + [(me, at(0, 1, 0))]
+    others += [(me, at(d, 0, 0)) for d in range(1, NX)] + [(me, at(0, 0, d)) for d in range(1, NY)]
     barrier = pltpu.get_barrier_semaphore()
     for other in others:
         pl.semaphore_signal(barrier, inc=1, device_id=other, device_id_type=MESH)
-
+    far = (me, at(0, 1, 0))
+
+    @pl.when(zh == 0)
+    def _():
+        pl.semaphore_signal(barrier, inc=1, device_id=far, device_id_type=MESH)
+
+    pairs = [
+        (inner_hbm, inner_ref), (value_hbm, value_ref), (taps_hbm, taps_ref), (outer_hbm, outer_ref),
+        (f1_hbm, f1), (f2_hbm, f2), (g_hbm, g), (tw_hbm, tw), (w_hbm, w),
+    ]
+    loads = [pltpu.make_async_copy(src, dst, load_sem.at[i]) for i, (src, dst) in enumerate(pairs)]
+    for load in loads:
+        load.start()
+
+    loads[0].wait()
+    loads[1].wait()
     signal = (inner_ref[...].astype(F32) * value_ref[...].astype(F32)).T
     hi, lo = halves(signal)
     send[:, 0:group] = hi.reshape(seq, group, rows)
     send[:, group : 2 * group] = lo.reshape(seq, group, rows)
+    loads[2].wait()
     send[:, 2 * group : 3 * group] = taps_ref[...].astype(F32).T.astype(BF16).reshape(seq, group, rows)
+    loads[3].wait()
     send_o[...] = outer_ref[...].astype(F32).T.astype(BF16).reshape(seq, group, rows)
-    pl.semaphore_wait(barrier, len(others))
+    pl.semaphore_wait(barrier, len(others) + zh)
+
+    @pl.when(zh == 1)
+    def _():
+        pl.semaphore_signal(far_sem, inc=1, device_id=far, device_id_type=MESH)
 
     def spread(src, dst, ss, rs):
         copies = []
@@ -127,7 +141,7 @@
     out_o = spread(send_o, got_o, o_ss, o_rs)
     got[me] = send[me]
     got_o[me] = send_o[me]
-    for load in loads[:4]:
+    for load in loads[4:8]:
         load.wait()
     for copy in out_a:
         copy.wait_recv()
@@ -140,11 +154,23 @@
         copy.wait_recv()
     gated = (got_o[...].reshape(n, rows).astype(F32) * conv).astype(BF16)
     send_g[...] = gated.reshape(seq, group, rows)
-    out_g = spread(send_g, got_g, g_ss, g_rs)
+    out_g = []
+    for i in range(seq - 1):
+        to = i + (i >= me).astype(jnp.int32)
+        copy = pltpu.make_async_remote_copy(
+            src_ref=send_g.at[to], dst_ref=got_g.at[me], send_sem=g_ss.at[to], recv_sem=g_rs.at[me],
+            device_id=(to, chan), device_id_type=MESH,
+        )
+        copy.start()
+        out_g.append(copy)
     got_g[me] = send_g[me]
-    loads[4].wait()
-    for copy in out_g:
-        copy.wait_recv()
+    loads[8].wait()
+    for i in range(seq - 1):
+        other = i + (i >= me).astype(jnp.int32)
+        pltpu.make_async_remote_copy(
+            src_ref=send_g.at[other], dst_ref=got_g.at[other], send_sem=g_ss.at[other], recv_sem=g_rs.at[other],
+            device_id=(other, chan), device_id_type=MESH,
+        ).wait_recv()
     mine = got_g[...].reshape(n, rows).astype(F32).T.astype(BF16)
 
     width = channels
@@ -157,6 +183,13 @@
         return copy
 
     order = [2, 1, 3, 0]
+
+    def start1(wave, h, d):
+        stage1[wave, h, d] = remote(
+            s1.at[wave, h, d - 1], r1.at[wave, h, d - 1], s1_ss.at[wave, h, d - 1], s1_rs.at[wave, h, d - 1],
+            d * (1 - h), 0, d * h,
+        )
+
     sent = []
     stage1 = {}
     for wave in range(2):
@@ -178,13 +211,9 @@
                     acc[wave, 1, :, dx * width : (dx + 1) * width] = block[half:]
                 else:
                     s1[wave, 1, dy - 1, :, dx * width : (dx + 1) * width] = block[half:].astype(BF16)
-            if first:
+            if first and wave == 0:
                 for h in range(2):
-                    stage1[wave, h, first] = remote(
-                        s1.at[wave, h, first - 1], r1.at[wave, h, first - 1],
-                        s1_ss.at[wave, h, first - 1], s1_rs.at[wave, h, first - 1],
-                        first * (1 - h), 0, first * h,
-                    )
+                    start1(wave, h, first)
     last = []
     for wave in range(2):
         stage2 = {}
@@ -205,17 +234,31 @@
                 else:
                     acc[wave, h, :, cols] = total
         sent += list(stage2.values())
+        if wave == 0:
+            for d in order[:3]:
+                for h in range(2):
+                    start1(1, h, d)
         for h in range(2):
             total = acc[wave, h, :, 0:width]
             for d in (1, 3, 2):
                 stage2[h, d].wait_recv()
                 total = total + r2[wave, h, d - 1].astype(F32)
             if wave == 0:
+                if h == 0:
+
+                    @pl.when(zh == 0)
+                    def _():
+                        pl.semaphore_wait(far_sem, 1)
+
                 zs[h] = total.astype(BF16)
-                last.append(remote(zs.at[h], zr.at[h], z_ss.at[h], z_rs.at[h], 0, 1, 0))
+                last.append(remote(zs.at[h], far_hbm.at[h], z_ss.at[h], z_rs.at[h], 0, 1, 0))
             else:
-                last[h].wait_recv()
-                out_ref[h * half : (h + 1) * half, :] = total + zr[h].astype(F32)
+                own[h * half : (h + 1) * half] = total
+    store = pltpu.make_async_copy(own, own_hbm, own_sem)
+    store.start()
+    for copy in last:
+        copy.wait_recv()
+    store.wait()
     for copy in out_a + out_o + out_g + list(stage1.values()) + sent + last:
         copy.wait_send()
 
@@ -226,10 +269,10 @@
     group, half = channels // seq, rows // 2
     f1, f2, g, tw = transform_constants(seq, rows, group)
     vmem, dma = pltpu.VMEM, pltpu.SemaphoreType.DMA
-    in_vmem = pl.BlockSpec(memory_space=pltpu.VMEM)
-    in_any = pl.BlockSpec(memory_space=pl.ANY)
+    in_hbm = pl.BlockSpec(memory_space=pltpu.HBM)
     peers = seq - 1
     scratch = [
+        *[vmem((rows, channels), BF16)] * 4,
         vmem((seq, 3 * group, rows), BF16), vmem((seq, group, rows), BF16),
         vmem((seq, 3 * group, rows), BF16), vmem((seq, group, rows), BF16),
         vmem((seq, group, rows), BF16), vmem((seq, group, rows), BF16),
@@ -237,19 +280,20 @@
         vmem((2, 2, half, 4 * channels), F32),
         vmem((2, 2, 3, half, 4 * channels), BF16), vmem((2, 2, 3, half, 4 * channels), BF16),
         vmem((2, 2, 3, half, channels), BF16), vmem((2, 2, 3, half, channels), BF16),
-        vmem((2, half, channels), BF16), vmem((2, half, channels), BF16),
-        dma((5,)), dma((peers,)), dma((peers,)), dma((peers,)), dma((peers,)), dma((peers,)), dma((peers,)),
+        vmem((2, half, channels), BF16), vmem((rows, channels), F32),
+        dma((9,)), dma(()), pltpu.SemaphoreType.REGULAR, dma((peers,)), dma((peers,)), dma((peers,)), dma((peers,)), dma((seq,)), dma((seq,)),
         dma((2, 2, 3)), dma((2, 2, 3)), dma((2, 2, 3)), dma((2, 2, 3)), dma((2,)), dma((2,)),
     ]
-    return pl.pallas_call(
+    own, far = pl.pallas_call(
         kernel,
-        out_shape=jax.ShapeDtypeStruct((rows, channels), F32),
-        in_specs=[in_vmem] * 4 + [in_any] * 5,
-        out_specs=in_vmem,
+        out_shape=(jax.ShapeDtypeStruct((rows, channels), F32), jax.ShapeDtypeStruct((2, half, channels), BF16)),
+        in_specs=[in_hbm] * 9,
+        out_specs=(in_hbm, in_hbm),
         scratch_shapes=scratch,
-        compiler_params=pltpu.CompilerParams(collective_id=0, has_side_effects=True, vmem_limit_bytes=48 * 2**20),
+        compiler_params=pltpu.CompilerParams(collective_id=0, has_side_effects=True, vmem_limit_bytes=62 * 2**20),
         name="hyena",
     )(inner_gate, value_in, outer_gate, filter_taps, out_weight, *(jnp.asarray(c) for c in (f1, f2, g, tw)))
+    return own + far.reshape(rows, channels).astype(F32)
 
 
 def solution(mesh):

time: 74.3 us -> 62.3 us (0.84)
  local copies, waits for them, and re-layouts: 10.2 us -> 0 us
  Pallas kernels: 63.6 us -> 60.6 us
  other arithmetic: 0 us -> 1.58 us
    unnamed x19 -> x0, local copies, waits for them, and re-layouts: 10.2 us -> none
    pallas_call x1, Pallas kernels: 63.6 us -> 60.6 us  [local(): pl.pallas_call(kernel, out_shape=(jax.ShapeDtypeStruct((rows, channels),...]
    add x0 -> x1, other arithmetic: none -> 1.58 us  [local(): return own + far.reshape(rows, channels).astype(F32)]
where the time goes in v2:
time: 62.3 us; the launch traced here: 62.2 us
  Pallas kernels  60.6 us (97%)
  other arithmetic  1.58 us (3%)
    pallas_call x1, Pallas kernels, local(): pl.pallas_call(kernel, out_shape=(jax.ShapeDtypeStruct((rows, channels),...  60.6 us
    add x1, other arithmetic, local(): return own + far.reshape(rows, channels).astype(F32)  1.58 us

profile of v2, /device:TPU:32, one launch (start us, length us, event | category | flops | bytes accessed | tf_op | source)
XLA Modules:
  0.0 62.2 jit_solution(13453909137313386848)
XLA Ops:
  0.0 60.6 %hyena.1 = (f32[128,256]{1,0:T(8,128)}, bf16[2,64,256]{2,1,0:T(8,128)(2,1)}) custom-call(bf16[128,256]{1,0:T(8,128)(2,1)} %inner_hbm.1, bf16[128,256]{1,0:T(8,128)(2,1)} %value_hbm.1, bf16[128,256]{1,0:T(8,128)(2,1)} %outer_hbm.1, bf16[128,256]{1,0:T(8,128)(2,1)} %taps_hbm.1, bf16[256,8192]{1,0:T(8,128)(2,1)} %w_hbm.1, ...), custom_call_target="tpu_custom_call" | custom-call | tf_op jit(solution)/shard_map/hyena/pallas_call | solution.py:287
  60.6 1.6 %convert_add_fusion = f32[128,256]{1,0:T(8,128)} fusion(f32[128,256]{1,0:T(8,128)} %get-tuple-element.7, bf16[2,64,256]{2,1,0:T(8,128)(2,1)} %get-tuple-element.8), kind=kLoop, calls=%fused_computation | loop fusion | flops 65536 | bytes 327680 | tf_op jit(solution)/shard_map/add | solution.py:296

commit v3 on v2

--- a/solution.py
+++ b/solution.py
@@ -77,8 +77,8 @@
 
 def kernel(
     inner_hbm, value_hbm, outer_hbm, taps_hbm, w_hbm, f1_hbm, f2_hbm, g_hbm, tw_hbm, own_hbm, far_hbm,
-    inner_ref, value_ref, outer_ref, taps_ref, send, send_o, got, got_o, send_g, got_g, w, f1, f2, g, tw, acc, s1, r1, s2, r2, zs, own,
-    load_sem, own_sem, far_sem, a_ss, a_rs, o_ss, o_rs, g_ss, g_rs, s1_ss, s1_rs, s2_ss, s2_rs, z_ss, z_rs,
+    inner_ref, value_ref, outer_ref, taps_ref, send, send_o, got, got_o, send_g, got_g, w, wxa, wxb, f1, f2, g, tw, mine, gx, acc0, acc1, s1, r1, s2, r2, zs, own,
+    load_sem, own_sem, far_sem, a_ss, a_rs, o_ss, o_rs, g_ss, g_rs, wa_ss, wa_rs, wb_ss, wb_rs, f_ss, f_rs, gx_ss, gx_rs, s1_ss, s1_rs, s2_ss, s2_rs, z_ss, z_rs,
 ):
     seq = lax.axis_size("seq")
     me, chan = lax.axis_index("seq"), lax.axis_index("chan")
@@ -137,8 +137,32 @@
             copies.append(copy)
         return copies
 
+    def remote(src, dst, ss, rs, dx=0, dz=0, dy=0, to=None):
+        copy = pltpu.make_async_remote_copy(
+            src_ref=src, dst_ref=dst, send_sem=ss, recv_sem=rs,
+            device_id=(me, at(dx, dz, dy)) if to is None else to, device_id_type=MESH,
+        )
+        copy.start()
+        return copy
+
     out_a = spread(send, got, a_ss, a_rs)
     out_o = spread(send_o, got_o, o_ss, o_rs)
+    order, width = [2, 1, 3, 0], channels
+    core = lax.rem(me, 2)
+    sibling = (me + 1 - 2 * core, chan)
+    part = pl.ds(pl.multiple_of(core * (channels // 2), channels // 2), channels // 2)
+    weights, onward = {}, []
+    loads[8].wait()
+    for d in order[:3]:
+        column = pl.multiple_of(((x + d) % NX * NZ + 1 - zh) * NY * width, NY * width)
+        weights[0, d] = remote(
+            w.at[part, pl.ds(column, NY * width)], wxa.at[d - 1, part], wa_ss.at[d - 1], wa_rs.at[d - 1], dx=d
+        )
+        for i in range(NX):
+            column = pl.multiple_of(((i * NZ + 1 - zh) * NY + (y + d) % NY) * width, width)
+            weights[1, d, i] = remote(
+                w.at[part, pl.ds(column, width)], wxb.at[d - 1, i, part], wb_ss.at[d - 1, i], wb_rs.at[d - 1, i], dy=d
+            )
     got[me] = send[me]
     got_o[me] = send_o[me]
     for load in loads[4:8]:
@@ -164,102 +188,105 @@
         copy.start()
         out_g.append(copy)
     got_g[me] = send_g[me]
-    loads[8].wait()
+    for d in order:
+        if d:
+            weights[0, d].wait_recv()
+            onward.append(remote(wxa.at[d - 1, part], wxa.at[d - 1, part], f_ss.at[0, d - 1], f_rs.at[0, d - 1], to=sibling))
+            for i in range(NX):
+                weights[1, d, i].wait_recv()
+            onward.append(remote(wxb.at[d - 1, :, part], wxb.at[d - 1, :, part], f_ss.at[1, d - 1], f_rs.at[1, d - 1], to=sibling))
     for i in range(seq - 1):
         other = i + (i >= me).astype(jnp.int32)
         pltpu.make_async_remote_copy(
             src_ref=send_g.at[other], dst_ref=got_g.at[other], send_sem=g_ss.at[other], recv_sem=g_rs.at[other],
             device_id=(other, chan), device_id_type=MESH,
         ).wait_recv()
-    mine = got_g[...].reshape(n, rows).astype(F32).T.astype(BF16)
-
-    width = channels
-
-    def remote(src, dst, ss, rs, dx, dz, dy):
-        copy = pltpu.make_async_remote_copy(
-            src_ref=src, dst_ref=dst, send_sem=ss, recv_sem=rs, device_id=(me, at(dx, dz, dy)), device_id_type=MESH
+    mine[...] = got_g[...].reshape(n, rows).astype(F32).T.astype(BF16)
+
+    gather, stage1, stage2, last = {}, {}, {}, []
+    for d in order[:3]:
+        for h in range(2):
+            gather[h, d] = remote(
+                mine.at[pl.ds(h * half, half)], gx.at[h, d - 1], gx_ss.at[h, d - 1], gx_rs.at[h, d - 1],
+                d * (1 - h), 0, d * h,
+            )
+    for i in range(4):
+        for h in range(2):
+            block = (x * NZ + 1 - zh) * NY + i if h == 0 else (i * NZ + 1 - zh) * NY + y
+            column = pl.multiple_of(block * width, width)
+            acc0[h, i] = mm(mine[h * half : (h + 1) * half], w[:, pl.ds(column, width)])
+    for dx in order:
+        for dy in order:
+            column = pl.multiple_of(at(dx, 0, dy) * width, width)
+            block = mm(mine[...], w[:, pl.ds(column, width)])
+            if dx == 0:
+                acc1[0, dy] = block[:half]
+            else:
+                s1[0, dx - 1, :, dy * width : (dy + 1) * width] = block[:half].astype(BF16)
+            if dy == 0:
+                acc1[1, dx] = block[half:]
+            else:
+                s1[1, dy - 1, :, dx * width : (dx + 1) * width] = block[half:].astype(BF16)
+    for copy in onward:
+        copy.wait_recv()
+    for d in (1, 3, 2):
+        for h in range(2):
+            gather[h, d].wait_recv()
+            for i in range(4):
+                block = wxa[d - 1, :, i * width : (i + 1) * width] if h == 0 else wxb[d - 1, i]
+                acc0[h, i] += mm(gx[h, d - 1], block)
+
+    def second(wave, h, d, total):
+        s2[wave, h, d - 1] = total.astype(BF16)
+        stage2[wave, h, d] = remote(
+            s2.at[wave, h, d - 1], r2.at[wave, h, d - 1], s2_ss.at[wave, h, d - 1], s2_rs.at[wave, h, d - 1],
+            d * h, 0, d * (1 - h),
         )
-        copy.start()
-        return copy
-
-    order = [2, 1, 3, 0]
-
-    def start1(wave, h, d):
-        stage1[wave, h, d] = remote(
-            s1.at[wave, h, d - 1], r1.at[wave, h, d - 1], s1_ss.at[wave, h, d - 1], s1_rs.at[wave, h, d - 1],
-            d * (1 - h), 0, d * h,
-        )
-
-    sent = []
-    stage1 = {}
-    for wave in range(2):
-        dz = 1 - wave
-        done = set()
-        for first in order:
-            todo = [(first, d) for d in order] + [(d, first) for d in order]
-            for dx, dy in todo:
-                if (dx, dy) in done:
-                    continue
-                done.add((dx, dy))
-                column = pl.multiple_of(at(dx, dz, dy) * width, width)
-                block = mm(mine, w[:, pl.ds(column, width)])
-                if dx == 0:
-                    acc[wave, 0, :, dy * width : (dy + 1) * width] = block[:half]
-                else:
-                    s1[wave, 0, dx - 1, :, dy * width : (dy + 1) * width] = block[:half].astype(BF16)
-                if dy == 0:
-                    acc[wave, 1, :, dx * width : (dx + 1) * width] = block[half:]
-                else:
-                    s1[wave, 1, dy - 1, :, dx * width : (dx + 1) * width] = block[half:].astype(BF16)
-            if first and wave == 0:
-                for h in range(2):
-                    start1(wave, h, first)
-    last = []
-    for wave in range(2):
-        stage2 = {}
-        for h in range(2):
-            for d in (1, 3, 2):
-                stage1[wave, h, d].wait_recv()
-            for d in order:
-                cols = slice(d * width, (d + 1) * width)
-                total = acc[wave, h, :, cols]
-                for e in range(3):
-                    total = total + r1[wave, h, e, :, cols].astype(F32)
-                if d:
-                    s2[wave, h, d - 1] = total.astype(BF16)
-                    stage2[h, d] = remote(
-                        s2.at[wave, h, d - 1], r2.at[wave, h, d - 1],
-                        s2_ss.at[wave, h, d - 1], s2_rs.at[wave, h, d - 1], d * h, 0, d * (1 - h),
-                    )
-                else:
-                    acc[wave, h, :, cols] = total
-        sent += list(stage2.values())
-        if wave == 0:
-            for d in order[:3]:
-                for h in range(2):
-                    start1(1, h, d)
-        for h in range(2):
-            total = acc[wave, h, :, 0:width]
-            for d in (1, 3, 2):
-                stage2[h, d].wait_recv()
-                total = total + r2[wave, h, d - 1].astype(F32)
-            if wave == 0:
-                if h == 0:
-
-                    @pl.when(zh == 0)
-                    def _():
-                        pl.semaphore_wait(far_sem, 1)
-
-                zs[h] = total.astype(BF16)
-                last.append(remote(zs.at[h], far_hbm.at[h], z_ss.at[h], z_rs.at[h], 0, 1, 0))
+
+    def finished(wave, h, total):
+        for d in (1, 3, 2):
+            stage2[wave, h, d].wait_recv()
+            total = total + r2[wave, h, d - 1].astype(F32)
+        return total
+
+    for d in order[:3]:
+        for h in range(2):
+            second(0, h, d, acc0[h, (y + d) % NY if h == 0 else (x + d) % NX])
+    for d in order[:3]:
+        for h in range(2):
+            stage1[h, d] = remote(
+                s1.at[h, d - 1], r1.at[h, d - 1], s1_ss.at[h, d - 1], s1_rs.at[h, d - 1], d * (1 - h), 0, d * h
+            )
+    for h in range(2):
+        total = finished(0, h, acc0[h, y if h == 0 else x])
+        if h == 0:
+
+            @pl.when(zh == 0)
+            def _():
+                pl.semaphore_wait(far_sem, 1)
+
+        zs[h] = total.astype(BF16)
+        last.append(remote(zs.at[h], far_hbm.at[h], z_ss.at[h], z_rs.at[h], 0, 1, 0))
+    for h in range(2):
+        for d in (1, 3, 2):
+            stage1[h, d].wait_recv()
+        for d in order:
+            total = acc1[h, d]
+            for e in range(3):
+                total = total + r1[h, e, :, d * width : (d + 1) * width].astype(F32)
+            if d:
+                second(1, h, d, total)
             else:
-                own[h * half : (h + 1) * half] = total
+                acc1[h, 0] = total
+    for h in range(2):
+        own[h * half : (h + 1) * half] = finished(1, h, acc1[h, 0])
     store = pltpu.make_async_copy(own, own_hbm, own_sem)
     store.start()
     for copy in last:
         copy.wait_recv()
     store.wait()
-    for copy in out_a + out_o + out_g + list(stage1.values()) + sent + last:
+    groups = (weights, gather, stage1, stage2)
+    for copy in out_a + out_o + out_g + onward + last + [copy for g in groups for copy in g.values()]:
         copy.wait_send()
 
 
@@ -276,13 +303,16 @@
         vmem((seq, 3 * group, rows), BF16), vmem((seq, group, rows), BF16),
         vmem((seq, 3 * group, rows), BF16), vmem((seq, group, rows), BF16),
         vmem((seq, group, rows), BF16), vmem((seq, group, rows), BF16),
-        vmem(out_weight.shape, BF16), vmem(f1.shape, BF16), vmem(f2.shape, BF16), vmem(g.shape, BF16), vmem(tw.shape, F32),
-        vmem((2, 2, half, 4 * channels), F32),
-        vmem((2, 2, 3, half, 4 * channels), BF16), vmem((2, 2, 3, half, 4 * channels), BF16),
+        vmem(out_weight.shape, BF16), vmem((3, channels, NY * channels), BF16), vmem((3, NX, channels, channels), BF16),
+        vmem(f1.shape, BF16), vmem(f2.shape, BF16), vmem(g.shape, BF16), vmem(tw.shape, F32),
+        vmem((rows, channels), BF16), vmem((2, 3, half, channels), BF16),
+        vmem((2, 4, half, channels), F32), vmem((2, 4, half, channels), F32),
+        vmem((2, 3, half, 4 * channels), BF16), vmem((2, 3, half, 4 * channels), BF16),
         vmem((2, 2, 3, half, channels), BF16), vmem((2, 2, 3, half, channels), BF16),
         vmem((2, half, channels), BF16), vmem((rows, channels), F32),
         dma((9,)), dma(()), pltpu.SemaphoreType.REGULAR, dma((peers,)), dma((peers,)), dma((peers,)), dma((peers,)), dma((seq,)), dma((seq,)),
-        dma((2, 2, 3)), dma((2, 2, 3)), dma((2, 2, 3)), dma((2, 2, 3)), dma((2,)), dma((2,)),
+        dma((3,)), dma((3,)), dma((3, 4)), dma((3, 4)), dma((2, 3)), dma((2, 3)), dma((2, 3)), dma((2, 3)),
+        dma((2, 3)), dma((2, 3)), dma((2, 2, 3)), dma((2, 2, 3)), dma((2,)), dma((2,)),
     ]
     own, far = pl.pallas_call(
         kernel,

time: 62.3 us -> 57.7 us (0.926)
  the two profiles are of different devices: /device:TPU:32 before, /device:TPU:6 now
where the time goes in v3:
time: 57.7 us; the launch traced here: 57.6 us
  Pallas kernels  56 us (97%)
  other arithmetic  1.58 us (3%)
    pallas_call x1, Pallas kernels, local(): pl.pallas_call(kernel, out_shape=(jax.ShapeDtypeStruct((rows, channels),...  56 us
    add x1, other arithmetic, local(): return own + far.reshape(rows, channels).astype(F32)  1.58 us

profile of v3, /device:TPU:6, one launch (start us, length us, event | category | flops | bytes accessed | tf_op | source)
XLA Modules:
  0.0 57.6 jit_solution(11683413127481441705)
XLA Ops:
  0.0 56.0 %hyena.1 = (f32[128,256]{1,0:T(8,128)}, bf16[2,64,256]{2,1,0:T(8,128)(2,1)}) custom-call(bf16[128,256]{1,0:T(8,128)(2,1)} %inner_hbm.1, bf16[128,256]{1,0:T(8,128)(2,1)} %value_hbm.1, bf16[128,256]{1,0:T(8,128)(2,1)} %outer_hbm.1, bf16[128,256]{1,0:T(8,128)(2,1)} %taps_hbm.1, bf16[256,8192]{1,0:T(8,128)(2,1)} %w_hbm.1, ...), custom_call_target="tpu_custom_call" | custom-call | tf_op jit(solution)/shard_map/hyena/pallas_call | solution.py:317
  56.0 1.6 %convert_add_fusion = f32[128,256]{1,0:T(8,128)} fusion(f32[128,256]{1,0:T(8,128)} %get-tuple-element.7, bf16[2,64,256]{2,1,0:T(8,128)(2,1)} %get-tuple-element.8), kind=kLoop, calls=%fused_computation | loop fusion | flops 65536 | bytes 327680 | tf_op jit(solution)/shard_map/add | solution.py:326

commit v4 on v3

--- a/solution.py
+++ b/solution.py
@@ -76,19 +76,26 @@
 
 
 def kernel(
-    inner_hbm, value_hbm, outer_hbm, taps_hbm, w_hbm, f1_hbm, f2_hbm, g_hbm, tw_hbm, own_hbm, far_hbm,
-    inner_ref, value_ref, outer_ref, taps_ref, send, send_o, got, got_o, send_g, got_g, w, wxa, wxb, f1, f2, g, tw, mine, gx, acc0, acc1, s1, r1, s2, r2, zs, own,
-    load_sem, own_sem, far_sem, a_ss, a_rs, o_ss, o_rs, g_ss, g_rs, wa_ss, wa_rs, wb_ss, wb_rs, f_ss, f_rs, gx_ss, gx_rs, s1_ss, s1_rs, s2_ss, s2_rs, z_ss, z_rs,
+    inner_hbm, value_hbm, outer_hbm, taps_hbm, w_hbm, f1_hbm, f2_hbm, g_hbm, tw_hbm, f1f_hbm, f2f_hbm, twf_hbm, own0_hbm, own1_hbm, far_hbm,
+    inner_ref, value_ref, outer_ref, taps_ref, send, send_o, got, got_o, got_f, got_fo, send_g, send_gf, got_g, w, wxa, wxb, f1, f2, g, tw, f1f, f2f, twf, mine, gx, acc0, acc1, s1, r1, s2, r2, zs, own,
+    load_sem, own_sem, far_sem, a_ss, a_rs, b_ss, b_rs, p_ss, p_rs, o_ss, o_rs, g_ss, g_rs, h_ss, h_rs, wa_ss, wa_rs, wb_ss, wb_rs, f_ss, f_rs, gx_ss, gx_rs, s1_ss, s1_rs, s2_ss, s2_rs, z_ss, z_rs,
 ):
     seq = lax.axis_size("seq")
     me, chan = lax.axis_index("seq"), lax.axis_index("chan")
-    x, zh, y = chan // (NZ * NY), chan // NY % NZ, chan % NY
-    rows, channels = own_hbm.shape
+    x, zh, y = lax.div(chan, NZ * NY), lax.rem(lax.div(chan, NY), NZ), lax.rem(chan, NY)
+    xs = [x] + [lax.rem(x + d, NX) for d in range(1, NX)]
+    ys = [y] + [lax.rem(y + d, NY) for d in range(1, NY)]
+    zs_of = [zh, 1 - zh]
+    flips = [(1 << b) * (1 - 2 * lax.rem(lax.div(me, 1 << b), 2)) for b in range(seq.bit_length() - 1)]
+
+    def flipped(bits):
+        return sum((flip for b, flip in enumerate(flips) if bits >> b & 1), me)
+    half, channels = own0_hbm.shape
+    rows = 2 * half
     group = channels // seq
-    half = rows // 2
 
     def at(dx, dz, dy):
-        return ((x + dx) % NX * NZ + (zh + dz) % NZ) * NY + (y + dy) % NY
+        return (xs[dx] * NZ + zs_of[dz]) * NY + ys[dy]
 
     others = [(lax.rem(me + k, seq), chan) for k in range(1, seq)]
     others += [(me, at(d, 0, 0)) for d in range(1, NX)] + [(me, at(0, 0, d)) for d in range(1, NY)]
@@ -104,6 +111,7 @@
     pairs = [
         (inner_hbm, inner_ref), (value_hbm, value_ref), (taps_hbm, taps_ref), (outer_hbm, outer_ref),
         (f1_hbm, f1), (f2_hbm, f2), (g_hbm, g), (tw_hbm, tw), (w_hbm, w),
+        (f1f_hbm, f1f), (f2f_hbm, f2f), (twf_hbm, twf),
     ]
     loads = [pltpu.make_async_copy(src, dst, load_sem.at[i]) for i, (src, dst) in enumerate(pairs)]
     for load in loads:
@@ -125,18 +133,6 @@
     def _():
         pl.semaphore_signal(far_sem, inc=1, device_id=far, device_id_type=MESH)
 
-    def spread(src, dst, ss, rs):
-        copies = []
-        for k in range(1, seq):
-            to = lax.rem(me + k, seq)
-            copy = pltpu.make_async_remote_copy(
-                src_ref=src.at[to], dst_ref=dst.at[me], send_sem=ss.at[k - 1], recv_sem=rs.at[k - 1],
-                device_id=(to, chan), device_id_type=MESH,
-            )
-            copy.start()
-            copies.append(copy)
-        return copies
-
     def remote(src, dst, ss, rs, dx=0, dz=0, dy=0, to=None):
         copy = pltpu.make_async_remote_copy(
             src_ref=src, dst_ref=dst, send_sem=ss, recv_sem=rs,
@@ -145,62 +141,154 @@
         copy.start()
         return copy
 
-    out_a = spread(send, got, a_ss, a_rs)
-    out_o = spread(send_o, got_o, o_ss, o_rs)
+    mid = seq // 2
+    first, second_half = me < mid, me >= mid
+
+    def to_first(k, gates=False):
+        to = flipped(k)
+        src, dst, ss, rs = (send_o, got_fo, p_ss, p_rs) if gates else (send, got_f, b_ss, b_rs)
+        return pltpu.make_async_remote_copy(
+            src_ref=src.at[pl.ds(2 * to, 2)], dst_ref=dst.at[me], send_sem=ss.at[k - 1], recv_sem=rs.at[k - 1],
+            device_id=(to, chan), device_id_type=MESH,
+        )
+
+    @pl.when(first)
+    def _():
+        for k in reversed(range(1, mid)):
+            to_first(k).start()
+        got_f[me] = send[pl.ds(2 * me, 2)]
+        got_fo[me] = send_o[pl.ds(2 * me, 2)]
+
+    def across(ks):
+        copies = []
+        for k in ks:
+            to = flipped(k)
+            copies.append(remote(send.at[to], got.at[me], a_ss.at[k - 1], a_rs.at[k - 1], to=(to, chan)))
+        return copies
+
+    out_a = across(reversed(range(mid, seq)))
+
+    @pl.when(first)
+    def _():
+        for k in reversed(range(1, mid)):
+            to_first(k, True).start()
+
+    out_a += across(reversed(range(1, mid)))
+    got[me] = send[me]
+
+    def outer_to(k):
+        to = flipped(k)
+        return pltpu.make_async_remote_copy(
+            src_ref=send_o.at[to], dst_ref=got_o.at[me - mid], send_sem=o_ss.at[k - 1], recv_sem=o_rs.at[me - mid],
+            device_id=(to, chan), device_id_type=MESH,
+        )
+
+    def outer_from(i):
+        return pltpu.make_async_remote_copy(
+            src_ref=send_o.at[i], dst_ref=got_o.at[i], send_sem=o_ss.at[i], recv_sem=o_rs.at[i],
+            device_id=(mid + i, chan), device_id_type=MESH,
+        )
+
+    @pl.when(second_half)
+    def _():
+        for k in reversed(range(1, seq)):
+            outer_to(k).start()
+        got_o[me - mid] = send_o[me]
+
     order, width = [2, 1, 3, 0], channels
     core = lax.rem(me, 2)
     sibling = (me + 1 - 2 * core, chan)
     part = pl.ds(pl.multiple_of(core * (channels // 2), channels // 2), channels // 2)
     weights, onward = {}, []
+
+    def pass_on(d):
+        weights[0, d].wait_recv()
+        onward.append(remote(wxa.at[d - 1, part], wxa.at[d - 1, part], f_ss.at[0, d - 1], f_rs.at[0, d - 1], to=sibling))
+        for i in range(NX):
+            weights[1, d, i].wait_recv()
+        onward.append(remote(wxb.at[d - 1, :, part], wxb.at[d - 1, :, part], f_ss.at[1, d - 1], f_rs.at[1, d - 1], to=sibling))
+
     loads[8].wait()
-    for d in order[:3]:
-        column = pl.multiple_of(((x + d) % NX * NZ + 1 - zh) * NY * width, NY * width)
+    for d in (1, 3, 2):
+        column = pl.multiple_of((xs[d] * NZ + 1 - zh) * NY * width, NY * width)
         weights[0, d] = remote(
             w.at[part, pl.ds(column, NY * width)], wxa.at[d - 1, part], wa_ss.at[d - 1], wa_rs.at[d - 1], dx=d
         )
         for i in range(NX):
-            column = pl.multiple_of(((i * NZ + 1 - zh) * NY + (y + d) % NY) * width, width)
+            column = pl.multiple_of(((i * NZ + 1 - zh) * NY + ys[d]) * width, width)
             weights[1, d, i] = remote(
                 w.at[part, pl.ds(column, width)], wxb.at[d - 1, i, part], wb_ss.at[d - 1, i], wb_rs.at[d - 1, i], dy=d
             )
-    got[me] = send[me]
-    got_o[me] = send_o[me]
-    for load in loads[4:8]:
+    for load in loads[4:8] + loads[9:]:
         load.wait()
+    n = seq * group
+
+    def back_first(to, source):
+        return pltpu.make_async_remote_copy(
+            src_ref=send_gf.at[to], dst_ref=got_g.at[pl.ds(2 * source, 2)], send_sem=h_ss.at[to], recv_sem=h_rs.at[source],
+            device_id=(to, chan), device_id_type=MESH,
+        )
+
+    def back_second(i, source):
+        return pltpu.make_async_remote_copy(
+            src_ref=send_g.at[i], dst_ref=got_g.at[source], send_sem=g_ss.at[i], recv_sem=g_rs.at[source],
+            device_id=(mid + i, chan), device_id_type=MESH,
+        )
+
+    @pl.when(first)
+    def _():
+        for k in range(1, mid):
+            to_first(k).wait_recv()
+        conv = convolve(
+            got_f[:, :, 0:group].reshape(n, rows), got_f[:, :, group : 2 * group].reshape(n, rows),
+            got_f[:, :, 2 * group : 3 * group].reshape(n, rows), f1f, f2f, g, twf,
+        )
+        for k in range(1, mid):
+            to_first(k, True).wait_recv()
+        gated = (got_fo[...].reshape(n, rows).astype(F32) * conv).astype(BF16)
+        send_gf[...] = gated.reshape(mid, 2, group, rows)
+        for i in range(mid - 1):
+            back_first(i + (i >= me).astype(jnp.int32), me).start()
+        got_g[pl.ds(2 * me, 2)] = send_gf[me]
+
+    pass_on(1)
+    pass_on(3)
     for copy in out_a:
         copy.wait_recv()
-    n = seq * group
     conv = convolve(
         got[:, 0:group].reshape(n, rows), got[:, group : 2 * group].reshape(n, rows),
         got[:, 2 * group : 3 * group].reshape(n, rows), f1, f2, g, tw,
     )
-    for copy in out_o:
-        copy.wait_recv()
-    gated = (got_o[...].reshape(n, rows).astype(F32) * conv).astype(BF16)
-    send_g[...] = gated.reshape(seq, group, rows)
-    out_g = []
-    for i in range(seq - 1):
-        to = i + (i >= me).astype(jnp.int32)
-        copy = pltpu.make_async_remote_copy(
-            src_ref=send_g.at[to], dst_ref=got_g.at[me], send_sem=g_ss.at[to], recv_sem=g_rs.at[me],
-            device_id=(to, chan), device_id_type=MESH,
-        )
-        copy.start()
-        out_g.append(copy)
-    got_g[me] = send_g[me]
-    for d in order:
-        if d:
-            weights[0, d].wait_recv()
-            onward.append(remote(wxa.at[d - 1, part], wxa.at[d - 1, part], f_ss.at[0, d - 1], f_rs.at[0, d - 1], to=sibling))
-            for i in range(NX):
-                weights[1, d, i].wait_recv()
-            onward.append(remote(wxb.at[d - 1, :, part], wxb.at[d - 1, :, part], f_ss.at[1, d - 1], f_rs.at[1, d - 1], to=sibling))
-    for i in range(seq - 1):
-        other = i + (i >= me).astype(jnp.int32)
-        pltpu.make_async_remote_copy(
-            src_ref=send_g.at[other], dst_ref=got_g.at[other], send_sem=g_ss.at[other], recv_sem=g_rs.at[other],
-            device_id=(other, chan), device_id_type=MESH,
-        ).wait_recv()
+    for i in range(mid):
+
+        @pl.when(me != mid + i)
+        def _():
+            outer_from(i).wait_recv()
+
+    gated = (got_o[...].reshape(n // 2, rows).astype(F32) * conv).astype(BF16)
+    send_g[...] = gated.reshape(mid, group, rows)
+    for i in range(mid):
+
+        @pl.when(me != mid + i)
+        def _():
+            back_second(i, me).start()
+
+    @pl.when(second_half)
+    def _():
+        got_g[me] = send_g[me - mid]
+
+    pass_on(2)
+
+    @pl.when(first)
+    def _():
+        for k in range(1, mid):
+            back_first(me, flipped(k)).wait_recv()
+
+    @pl.when(second_half)
+    def _():
+        for k in range(1, seq):
+            back_second(me - mid, flipped(k)).wait_recv()
+
     mine[...] = got_g[...].reshape(n, rows).astype(F32).T.astype(BF16)
 
     gather, stage1, stage2, last = {}, {}, {}, []
@@ -251,7 +339,7 @@
 
     for d in order[:3]:
         for h in range(2):
-            second(0, h, d, acc0[h, (y + d) % NY if h == 0 else (x + d) % NX])
+            second(0, h, d, acc0[h, ys[d] if h == 0 else xs[d]])
     for d in order[:3]:
         for h in range(2):
             stage1[h, d] = remote(
@@ -278,15 +366,36 @@
                 second(1, h, d, total)
             else:
                 acc1[h, 0] = total
+    stores = []
     for h in range(2):
-        own[h * half : (h + 1) * half] = finished(1, h, acc1[h, 0])
-    store = pltpu.make_async_copy(own, own_hbm, own_sem)
-    store.start()
+        own[h] = finished(1, h, acc1[h, 0])
+        stores.append(pltpu.make_async_copy(own.at[h], (own0_hbm, own1_hbm)[h], own_sem.at[h]))
+        stores[h].start()
     for copy in last:
         copy.wait_recv()
-    store.wait()
+    for store in stores:
+        store.wait()
     groups = (weights, gather, stage1, stage2)
-    for copy in out_a + out_o + out_g + onward + last + [copy for g in groups for copy in g.values()]:
+    @pl.when(first)
+    def _():
+        for k in range(1, mid):
+            to_first(k).wait_send()
+            to_first(k, True).wait_send()
+        for i in range(mid - 1):
+            back_first(i + (i >= me).astype(jnp.int32), me).wait_send()
+
+    @pl.when(second_half)
+    def _():
+        for k in range(1, seq):
+            outer_to(k).wait_send()
+
+    for i in range(mid):
+
+        @pl.when(me != mid + i)
+        def _():
+            back_second(i, me).wait_send()
+
+    for copy in out_a + onward + last + [copy for g in groups for copy in g.values()]:
         copy.wait_send()
 
 
@@ -295,35 +404,40 @@
     seq = lax.axis_size("seq")
     group, half = channels // seq, rows // 2
     f1, f2, g, tw = transform_constants(seq, rows, group)
+    f2 = f2[:, f2.shape[1] // 2 :]
+    f1f, f2f, _, twf = transform_constants(seq // 2, rows, 2 * group)
     vmem, dma = pltpu.VMEM, pltpu.SemaphoreType.DMA
-    in_hbm = pl.BlockSpec(memory_space=pltpu.HBM)
-    peers = seq - 1
+    in_hbm, in_any = pl.BlockSpec(memory_space=pltpu.HBM), pl.BlockSpec(memory_space=pl.ANY)
+    peers, mid = seq - 1, seq // 2
     scratch = [
         *[vmem((rows, channels), BF16)] * 4,
         vmem((seq, 3 * group, rows), BF16), vmem((seq, group, rows), BF16),
-        vmem((seq, 3 * group, rows), BF16), vmem((seq, group, rows), BF16),
-        vmem((seq, group, rows), BF16), vmem((seq, group, rows), BF16),
+        vmem((seq, 3 * group, rows), BF16), vmem((mid, group, rows), BF16),
+        vmem((mid, 2, 3 * group, rows), BF16), vmem((mid, 2, group, rows), BF16),
+        vmem((mid, group, rows), BF16), vmem((mid, 2, group, rows), BF16), vmem((seq, group, rows), BF16),
         vmem(out_weight.shape, BF16), vmem((3, channels, NY * channels), BF16), vmem((3, NX, channels, channels), BF16),
         vmem(f1.shape, BF16), vmem(f2.shape, BF16), vmem(g.shape, BF16), vmem(tw.shape, F32),
+        vmem(f1f.shape, BF16), vmem(f2f.shape, BF16), vmem(twf.shape, F32),
         vmem((rows, channels), BF16), vmem((2, 3, half, channels), BF16),
         vmem((2, 4, half, channels), F32), vmem((2, 4, half, channels), F32),
         vmem((2, 3, half, 4 * channels), BF16), vmem((2, 3, half, 4 * channels), BF16),
         vmem((2, 2, 3, half, channels), BF16), vmem((2, 2, 3, half, channels), BF16),
-        vmem((2, half, channels), BF16), vmem((rows, channels), F32),
-        dma((9,)), dma(()), pltpu.SemaphoreType.REGULAR, dma((peers,)), dma((peers,)), dma((peers,)), dma((peers,)), dma((seq,)), dma((seq,)),
+        vmem((2, half, channels), BF16), vmem((2, half, channels), F32),
+        dma((12,)), dma((2,)), pltpu.SemaphoreType.REGULAR, dma((peers,)), dma((peers,)), *[dma((mid - 1,))] * 4, dma((peers,)), dma((mid,)),
+        dma((mid,)), dma((seq,)), dma((mid,)), dma((mid,)),
         dma((3,)), dma((3,)), dma((3, 4)), dma((3, 4)), dma((2, 3)), dma((2, 3)), dma((2, 3)), dma((2, 3)),
         dma((2, 3)), dma((2, 3)), dma((2, 2, 3)), dma((2, 2, 3)), dma((2,)), dma((2,)),
     ]
-    own, far = pl.pallas_call(
+    *own, far = pl.pallas_call(
         kernel,
-        out_shape=(jax.ShapeDtypeStruct((rows, channels), F32), jax.ShapeDtypeStruct((2, half, channels), BF16)),
-        in_specs=[in_hbm] * 9,
-        out_specs=(in_hbm, in_hbm),
+        out_shape=(*[jax.ShapeDtypeStruct((half, channels), F32)] * 2, jax.ShapeDtypeStruct((2, half, channels), BF16)),
+        in_specs=[in_hbm] * 12,
+        out_specs=(in_any,) * 3,
         scratch_shapes=scratch,
-        compiler_params=pltpu.CompilerParams(collective_id=0, has_side_effects=True, vmem_limit_bytes=62 * 2**20),
+        compiler_params=pltpu.CompilerParams(collective_id=0, has_side_effects=True, vmem_limit_bytes=5372 * 2**20 // 100),
         name="hyena",
-    )(inner_gate, value_in, outer_gate, filter_taps, out_weight, *(jnp.asarray(c) for c in (f1, f2, g, tw)))
-    return own + far.reshape(rows, channels).astype(F32)
+    )(inner_gate, value_in, outer_gate, filter_taps, out_weight, *(jnp.asarray(c) for c in (f1, f2, g, tw, f1f, f2f, twf)))
+    return jnp.concatenate([part + far[h].astype(F32) for h, part in enumerate(own)], 0)
 
 
 def solution(mesh):

time: 57.7 us -> 54.5 us (0.945)
  the two profiles are of different devices: /device:TPU:6 before, /device:TPU:128 now
where the time goes in v4:
time: 54.5 us; the launch traced here: 54.3 us
  Pallas kernels  53.7 us (99%)
  other arithmetic  0.68 us (1%)
    pallas_call x1, Pallas kernels, local(): pl.pallas_call(kernel, out_shape=(*[jax.ShapeDtypeStruct((half, channels)...  53.7 us

profile of v4, /device:TPU:128, one launch (start us, length us, event | category | flops | bytes accessed | tf_op | source)
XLA Modules:
  0.0 54.3 jit_solution(2499705279839208326)
XLA Ops:
  0.0 53.7 %hyena.1 = (f32[64,256]{1,0:T(8,128)S(1)}, f32[64,256]{1,0:T(8,128)S(1)}, bf16[2,64,256]{2,1,0:T(8,128)(2,1)S(1)}) custom-call(bf16[128,256]{1,0:T(8,128)(2,1)} %inner_hbm.1, bf16[128,256]{1,0:T(8,128)(2,1)} %value_hbm.1, bf16[128,256]{1,0:T(8,128)(2,1)} %outer_hbm.1, bf16[128,256]{1,0:T(8,128)(2,1)} %taps_hbm.1, bf16[256,8192]{1,0:T(8,128)(2,1)} %w_hbm.1, ...), custom_call_target="tpu_custom_call" | custom-call | tf_op jit(solution)/shard_map/hyena/pallas_call | solution.py:431
  53.7 0.7 %pad_maximum_fusion = f32[128,256]{1,0:T(8,128)} fusion(f32[64,256]{1,0:T(8,128)S(1)} %get-tuple-element.12, f32[64,256]{1,0:T(8,128)S(1)} %get-tuple-element.11), kind=kLoop, calls=%fused_computation | loop fusion | flops 32768 | bytes 262144 | tf_op jit(solution)/shard_map/concatenate | solution.py:440
  (1 shorter events, 0.0 us)

commit v5 on v4

--- a/solution.py
+++ b/solution.py
@@ -144,6 +144,10 @@
     mid = seq // 2
     first, second_half = me < mid, me >= mid
 
+    def block_of(device):
+        return 2 * lax.rem(device, mid) + lax.div(device, mid)
+
+
     def to_first(k, gates=False):
         to = flipped(k)
         src, dst, ss, rs = (send_o, got_fo, p_ss, p_rs) if gates else (send, got_f, b_ss, b_rs)
@@ -159,41 +163,43 @@
         got_f[me] = send[pl.ds(2 * me, 2)]
         got_fo[me] = send_o[pl.ds(2 * me, 2)]
 
-    def across(ks):
-        copies = []
-        for k in ks:
-            to = flipped(k)
-            copies.append(remote(send.at[to], got.at[me], a_ss.at[k - 1], a_rs.at[k - 1], to=(to, chan)))
-        return copies
-
-    out_a = across(reversed(range(mid, seq)))
-
-    @pl.when(first)
-    def _():
-        for k in reversed(range(1, mid)):
-            to_first(k, True).start()
-
-    out_a += across(reversed(range(1, mid)))
-    got[me] = send[me]
+    def full_to(k):
+        to = flipped(k)
+        return pltpu.make_async_remote_copy(
+            src_ref=send.at[block_of(to)], dst_ref=got.at[me], send_sem=a_ss.at[k - 1], recv_sem=a_rs.at[k - 1],
+            device_id=(to, chan), device_id_type=MESH,
+        )
 
     def outer_to(k):
         to = flipped(k)
         return pltpu.make_async_remote_copy(
-            src_ref=send_o.at[to], dst_ref=got_o.at[me - mid], send_sem=o_ss.at[k - 1], recv_sem=o_rs.at[me - mid],
+            src_ref=send_o.at[block_of(to)], dst_ref=got_o.at[me - mid], send_sem=o_ss.at[k - 1], recv_sem=o_rs.at[me - mid],
             device_id=(to, chan), device_id_type=MESH,
         )
+
+    across, near = list(reversed(range(mid, seq))), list(reversed(range(1, mid)))
+    for k in across:
+        full_to(k).start()
+
+    @pl.when(first)
+    def _():
+        for k in near:
+            to_first(k, True).start()
+
+    @pl.when(second_half)
+    def _():
+        for k in near:
+            full_to(k).start()
+        for k in across + near:
+            outer_to(k).start()
+        got[me] = send[block_of(me)]
+        got_o[me - mid] = send_o[block_of(me)]
 
     def outer_from(i):
         return pltpu.make_async_remote_copy(
             src_ref=send_o.at[i], dst_ref=got_o.at[i], send_sem=o_ss.at[i], recv_sem=o_rs.at[i],
             device_id=(mid + i, chan), device_id_type=MESH,
         )
-
-    @pl.when(second_half)
-    def _():
-        for k in reversed(range(1, seq)):
-            outer_to(k).start()
-        got_o[me - mid] = send_o[me]
 
     order, width = [2, 1, 3, 0], channels
     core = lax.rem(me, 2)
@@ -231,7 +237,7 @@
 
     def back_second(i, source):
         return pltpu.make_async_remote_copy(
-            src_ref=send_g.at[i], dst_ref=got_g.at[source], send_sem=g_ss.at[i], recv_sem=g_rs.at[source],
+            src_ref=send_g.at[i], dst_ref=got_g.at[block_of(source)], send_sem=g_ss.at[i], recv_sem=g_rs.at[source],
             device_id=(mid + i, chan), device_id_type=MESH,
         )
 
@@ -249,12 +255,19 @@
         send_gf[...] = gated.reshape(mid, 2, group, rows)
         for i in range(mid - 1):
             back_first(i + (i >= me).astype(jnp.int32), me).start()
+        got[:mid] = got_f[:, 0]
         got_g[pl.ds(2 * me, 2)] = send_gf[me]
 
     pass_on(1)
     pass_on(3)
-    for copy in out_a:
-        copy.wait_recv()
+    for k in across:
+        full_to(k).wait_recv()
+
+    @pl.when(second_half)
+    def _():
+        for k in near:
+            full_to(k).wait_recv()
+
     conv = convolve(
         got[:, 0:group].reshape(n, rows), got[:, group : 2 * group].reshape(n, rows),
         got[:, 2 * group : 3 * group].reshape(n, rows), f1, f2, g, tw,
@@ -275,7 +288,7 @@
 
     @pl.when(second_half)
     def _():
-        got_g[me] = send_g[me - mid]
+        got_g[block_of(me)] = send_g[me - mid]
 
     pass_on(2)
 
@@ -315,6 +328,11 @@
                 acc1[1, dx] = block[half:]
             else:
                 s1[1, dy - 1, :, dx * width : (dx + 1) * width] = block[half:].astype(BF16)
+    for d in order[:1]:
+        for h in range(2):
+            stage1[h, d] = remote(
+                s1.at[h, d - 1], r1.at[h, d - 1], s1_ss.at[h, d - 1], s1_rs.at[h, d - 1], d * (1 - h), 0, d * h
+            )
     for copy in onward:
         copy.wait_recv()
     for d in (1, 3, 2):
@@ -340,7 +358,7 @@
     for d in order[:3]:
         for h in range(2):
             second(0, h, d, acc0[h, ys[d] if h == 0 else xs[d]])
-    for d in order[:3]:
+    for d in order[1:3]:
         for h in range(2):
             stage1[h, d] = remote(
                 s1.at[h, d - 1], r1.at[h, d - 1], s1_ss.at[h, d - 1], s1_rs.at[h, d - 1], d * (1 - h), 0, d * h
@@ -386,8 +404,13 @@
 
     @pl.when(second_half)
     def _():
-        for k in range(1, seq):
+        for k in across + near:
             outer_to(k).wait_send()
+        for k in near:
+            full_to(k).wait_send()
+
+    for k in across:
+        full_to(k).wait_send()
 
     for i in range(mid):
 
@@ -395,7 +418,7 @@
         def _():
             back_second(i, me).wait_send()
 
-    for copy in out_a + onward + last + [copy for g in groups for copy in g.values()]:
+    for copy in onward + last + [copy for g in groups for copy in g.values()]:
         copy.wait_send()
 
 

time: 54.5 us -> 50.7 us (0.930)
  the two profiles are of different devices: /device:TPU:128 before, /device:TPU:6 now
where the time goes in v5:
time: 50.7 us; the launch traced here: 50.1 us
  Pallas kernels  49.4 us (97%)
  other arithmetic  0.68 us (1%)
    pallas_call x1, Pallas kernels, local(): pl.pallas_call(kernel, out_shape=(*[jax.ShapeDtypeStruct((half, channels)...  49.4 us

profile of v5, /device:TPU:6, one launch (start us, length us, event | category | flops | bytes accessed | tf_op | source)
XLA Modules:
  0.0 50.1 jit_solution(4072209975503584273)
XLA Ops:
  0.0 49.4 %hyena.1 = (f32[64,256]{1,0:T(8,128)S(1)}, f32[64,256]{1,0:T(8,128)S(1)}, bf16[2,64,256]{2,1,0:T(8,128)(2,1)S(1)}) custom-call(bf16[128,256]{1,0:T(8,128)(2,1)} %inner_hbm.1, bf16[128,256]{1,0:T(8,128)(2,1)} %value_hbm.1, bf16[128,256]{1,0:T(8,128)(2,1)} %outer_hbm.1, bf16[128,256]{1,0:T(8,128)(2,1)} %taps_hbm.1, bf16[256,8192]{1,0:T(8,128)(2,1)} %w_hbm.1, ...), custom_call_target="tpu_custom_call" | custom-call | tf_op jit(solution)/shard_map/hyena/pallas_call | solution.py:454
  49.4 0.7 %pad_maximum_fusion = f32[128,256]{1,0:T(8,128)} fusion(f32[64,256]{1,0:T(8,128)S(1)} %get-tuple-element.12, f32[64,256]{1,0:T(8,128)S(1)} %get-tuple-element.11), kind=kLoop, calls=%fused_computation | loop fusion | flops 32768 | bytes 262144 | tf_op jit(solution)/shard_map/concatenate | solution.py:463
  (1 shorter events, 0.0 us)

commit v6 on v5

--- a/solution.py
+++ b/solution.py
@@ -97,7 +97,7 @@
     def at(dx, dz, dy):
         return (xs[dx] * NZ + zs_of[dz]) * NY + ys[dy]
 
-    others = [(lax.rem(me + k, seq), chan) for k in range(1, seq)]
+    others = [(flipped(k), chan) for k in reversed(range(1, seq))]
     others += [(me, at(d, 0, 0)) for d in range(1, NX)] + [(me, at(0, 0, d)) for d in range(1, NY)]
     barrier = pltpu.get_barrier_semaphore()
     for other in others:
@@ -363,6 +363,31 @@
             stage1[h, d] = remote(
                 s1.at[h, d - 1], r1.at[h, d - 1], s1_ss.at[h, d - 1], s1_rs.at[h, d - 1], d * (1 - h), 0, d * h
             )
+    @pl.when(first)
+    def _():
+        for k in range(1, mid):
+            to_first(k).wait_send()
+            to_first(k, True).wait_send()
+        for i in range(mid - 1):
+            back_first(i + (i >= me).astype(jnp.int32), me).wait_send()
+
+    @pl.when(second_half)
+    def _():
+        for k in across + near:
+            outer_to(k).wait_send()
+        for k in near:
+            full_to(k).wait_send()
+
+    for k in across:
+        full_to(k).wait_send()
+
+    for i in range(mid):
+
+        @pl.when(me != mid + i)
+        def _():
+            back_second(i, me).wait_send()
+    for copy in onward + list(weights.values()) + list(gather.values()):
+        copy.wait_send()
     for h in range(2):
         total = finished(0, h, acc0[h, y if h == 0 else x])
         if h == 0:
@@ -389,36 +414,13 @@
         own[h] = finished(1, h, acc1[h, 0])
         stores.append(pltpu.make_async_copy(own.at[h], (own0_hbm, own1_hbm)[h], own_sem.at[h]))
         stores[h].start()
+    for copy in list(stage1.values()) + list(stage2.values()):
+        copy.wait_send()
     for copy in last:
         copy.wait_recv()
     for store in stores:
         store.wait()
-    groups = (weights, gather, stage1, stage2)
-    @pl.when(first)
-    def _():
-        for k in range(1, mid):
-            to_first(k).wait_send()
-            to_first(k, True).wait_send()
-        for i in range(mid - 1):
-            back_first(i + (i >= me).astype(jnp.int32), me).wait_send()
-
-    @pl.when(second_half)
-    def _():
-        for k in across + near:
-            outer_to(k).wait_send()
-        for k in near:
-            full_to(k).wait_send()
-
-    for k in across:
-        full_to(k).wait_send()
-
-    for i in range(mid):
-
-        @pl.when(me != mid + i)
-        def _():
-            back_second(i, me).wait_send()
-
-    for copy in onward + last + [copy for g in groups for copy in g.values()]:
+    for copy in last:
         copy.wait_send()
 
 

time: 50.7 us -> 50.4 us (level)
  no operation moved by 1% of the time
where the time goes in v6:
time: 50.4 us; the launch traced here: 49.8 us
  Pallas kernels  49.1 us (97%)
  other arithmetic  0.68 us (1%)
    pallas_call x1, Pallas kernels, local(): pl.pallas_call(kernel, out_shape=(*[jax.ShapeDtypeStruct((half, channels)...  49.1 us

profile of v6, /device:TPU:6, one launch (start us, length us, event | category | flops | bytes accessed | tf_op | source)
XLA Modules:
  0.0 49.8 jit_solution(9124674652488259158)
XLA Ops:
  0.0 49.1 %hyena.1 = (f32[64,256]{1,0:T(8,128)S(1)}, f32[64,256]{1,0:T(8,128)S(1)}, bf16[2,64,256]{2,1,0:T(8,128)(2,1)S(1)}) custom-call(bf16[128,256]{1,0:T(8,128)(2,1)} %inner_hbm.1, bf16[128,256]{1,0:T(8,128)(2,1)} %value_hbm.1, bf16[128,256]{1,0:T(8,128)(2,1)} %outer_hbm.1, bf16[128,256]{1,0:T(8,128)(2,1)} %taps_hbm.1, bf16[256,8192]{1,0:T(8,128)(2,1)} %w_hbm.1, ...), custom_call_target="tpu_custom_call" | custom-call | tf_op jit(solution)/shard_map/hyena/pallas_call | solution.py:456
  49.1 0.7 %pad_maximum_fusion = f32[128,256]{1,0:T(8,128)} fusion(f32[64,256]{1,0:T(8,128)S(1)} %get-tuple-element.12, f32[64,256]{1,0:T(8,128)S(1)} %get-tuple-element.11), kind=kLoop, calls=%fused_computation | loop fusion | flops 32768 | bytes 262144 | tf_op jit(solution)/shard_map/concatenate | solution.py:465
  (1 shorter events, 0.0 us)
